TPU v7x, 256 devices: a whole 4x4x8 slice. The times are simulated.
256 devices in a mesh: lat: 16 (over z_lo, y, core), lev: 4 (over x), ocn: 4 (over z_hi).
Axes of the slice: x: 4, y: 4, z: 8 (z_hi: 4, z_lo: 2; z = z_hi * 2 + z_lo), core: 2. Of those that a mesh axis runs over, the one named last changes fastest.
Arguments:
- atmos_fields: bfloat16 [2, 24, 2560, 5632], P(None, 'lev', ('lat', 'ocn')), may hold values from -6 to 6
- lat_points: int32 [2560], P(('lat', 'ocn')), may hold values from 20 to 5632, as said below
- wave_order: int32 [256], replicated, may hold values from 0 to 255, each once
- legendre: bfloat16 [256, 2560, 1536], P(('lat', 'ocn'), None, 'lev'), may hold values from -0.125 to 0.125
- column_weight: bfloat16 [2, 24], P(None, 'lev'), may hold values from -1.25 to 1.25
- block_remap: int32 [2560, 44], P(('lat', 'ocn'), 'lev'), may hold values from 0 to 17407, as said below
- ocean_temp: float32 [1024, 2176], P(('lat', 'ocn')), may hold values from -6 to 6
- ocean_salt: float32 [1024, 2176], P(('lat', 'ocn')), may hold values from -6 to 6
- sea_mask: int32 [1024, 17], P(('lat', 'ocn')), may hold values 0 or 1
Outputs:
- spectra: float32 [256, 96, 1536], P(('lat', 'ocn'), None, 'lev')
- temp_next: float32 [1024, 2176], P(('lat', 'ocn'))
- salt_next: float32 [1024, 2176], P(('lat', 'ocn'))
- surface_temp: float32 [2560, 5632], P(('lat', 'ocn'), 'lev')
Inputs may be any that keep to these rules, and one draw needn't show every extreme that they name: `lat_points`: a multiple of 4 for every latitude row. `wave_order`: each wavenumber appears once. `block_remap`: the blocks of latitude band g (rows g * 40 onward) name tiles of ocean sections g - 1, g or g + 1 only; section g holds tiles g * 16 * 17 onward, in row order.
All inputs are finite; a program needn't handle non-finite values. No bound on the sum of `sea_mask` on one device may be relied on, other than what follows from the above.
Results may differ from a plain program's by a relative error of at most 0.0037.
Values may be sent and summed in bfloat16 or wider, within the bound.
A program may use at most 128 MiB of HBM per device.

v0:
```python
import math

import jax
import jax.numpy as jnp
from jax import lax
from jax.sharding import PartitionSpec as P

FIELDS = 2
BLOCK = 128


FULL_TURN = 2.0 * math.pi
DIFFUSION = 0.2
COUPLING = 0.5


def with_halo(cells, sides, width):
    for axis, dim in sides:
        count = lax.axis_size(axis)
        ends = count - 1
        head = lax.slice_in_dim(cells, 0, width, axis=dim)
        tail = lax.slice_in_dim(cells, cells.shape[dim] - width, cells.shape[dim], axis=dim)
        cells = jnp.concatenate(
            [
                lax.ppermute(tail, axis, [(i, (i + 1) % count) for i in range(ends)]),
                cells,
                lax.ppermute(head, axis, [((i + 1) % count, i) for i in range(ends)]),
            ],
            axis=dim,
        )
    return cells


def fourier_table(wave_order, length):
    points = jnp.arange(length, dtype=jnp.int32)
    phase = wave_order[None, :] * points[:, None] % length
    angle = phase.astype(jnp.float32) * (FULL_TURN / length)
    table = jnp.concatenate([jnp.cos(angle), -jnp.sin(angle)], axis=1).astype(jnp.bfloat16)
    return (table, points)


def body(
    atmos_fields,
    lat_points,
    wave_order,
    legendre,
    column_weight,
    block_remap,
    ocean_temp,
    ocean_salt,
    sea_mask,
):
    nfields, lev_dev, lat_band, lon_count = atmos_fields.shape
    wave_count = wave_order.shape[0]
    table, points = fourier_table(wave_order, lon_count)
    point_mask = points[None, :] < lat_points[:, None]
    masked = jnp.where(point_mask[None, None], atmos_fields, jnp.zeros((), jnp.bfloat16))
    inverse_root = 1.0 / jnp.sqrt(lat_points.astype(jnp.float32))
    weights = jnp.where(
        2 * wave_order[None, :] < lat_points[:, None],
        inverse_root[:, None],
        jnp.zeros((), jnp.float32),
    )
    field_count = masked.shape[0]
    raw_sums = jnp.dot(masked.reshape(-1, lon_count), table, preferred_element_type=jnp.float32)
    raw_sums = raw_sums.reshape(field_count, lev_dev, lat_band, 2, wave_count)
    coeffs = (raw_sums * weights[None, None, :, None, :]).astype(jnp.bfloat16)
    regrouped = lax.all_to_all(
        coeffs.transpose(4, 1, 0, 3, 2).reshape(wave_count, lev_dev * field_count * 2, lat_band),
        ("lat", "ocn"),
        split_axis=0,
        concat_axis=2,
        tiled=True,
    )
    spectra = jnp.einsum(
        "srj,sjd->srd",
        lax.all_gather(regrouped, "lev", axis=1, tiled=True),
        legendre,
        preferred_element_type=jnp.float32,
    )
    ocean_rows, ocean_cols = ocean_temp.shape
    tile_count = ocean_rows * ocean_cols // BLOCK
    band_index = lax.axis_index(("lat", "ocn"))
    targets = block_remap.reshape(-1)
    local_slot = (targets // tile_count - band_index + 1) * tile_count + targets % tile_count
    partial_sum = jnp.einsum(
        "ql,qljk->qjk", column_weight, masked, preferred_element_type=jnp.float32
    )
    quarter = lon_count // lax.axis_size("lev")
    totals = lax.psum(partial_sum, "lev")
    own_flux = lax.dynamic_slice_in_dim(totals, lax.axis_index("lev") * quarter, quarter, 2)
    block_rows = (
        own_flux.reshape(FIELDS, lat_band, quarter // BLOCK, BLOCK)
        .transpose(1, 2, 0, 3)
        .reshape(-1, FIELDS * BLOCK)
    )
    outgoing = jax.ops.segment_sum(block_rows, local_slot, num_segments=3 * tile_count)
    widened = with_halo(outgoing, ((("lat", "ocn"), 0),), tile_count)
    arrived = (
        widened[:tile_count] + widened[2 * tile_count : 3 * tile_count] + widened[4 * tile_count :]
    )
    tile_sums = lax.psum(arrived, "lev")
    forcing = (
        tile_sums.reshape(ocean_rows, ocean_cols // BLOCK, FIELDS, BLOCK)
        .transpose(2, 0, 1, 3)
        .reshape(FIELDS, ocean_rows, ocean_cols)
    )
    sea_cells = (
        jnp.broadcast_to(sea_mask[:, :, None], (ocean_rows, ocean_cols // BLOCK, BLOCK))
        .reshape(ocean_rows, ocean_cols)
        .astype(jnp.float32)
    )
    ocean_state = jnp.stack([ocean_temp, ocean_salt])
    padded = with_halo(ocean_state, ((("lat", "ocn"), 1),), 1)
    laplace = (
        padded[:, 2:]
        + padded[:, :-2]
        + jnp.roll(ocean_state, 1, 2)
        + jnp.roll(ocean_state, -1, 2)
        - 4.0 * ocean_state
    )
    updated = ocean_state + DIFFUSION * laplace + COUPLING * sea_cells[None] * forcing
    temp_next = updated[0]
    salt_next = updated[1]
    returned = with_halo(temp_next, ((("lat", "ocn"), 0),), ocean_rows)
    tiles_near = returned.reshape(3 * tile_count, BLOCK)
    surface = jnp.take(tiles_near, local_slot, axis=0).reshape(lat_band, quarter)
    own_points = lax.axis_index("lev") * quarter + jnp.arange(quarter, dtype=jnp.int32)
    surface_temp = jnp.where(
        own_points[None, :] < lat_points[:, None], surface, jnp.zeros((), jnp.float32)
    )
    return (spectra, temp_next, salt_next, surface_temp)


def solution(mesh):
    placed = (
        P(None, "lev", ("lat", "ocn"), None),
        P(("lat", "ocn")),
        P(),
        P(("lat", "ocn"), None, "lev"),
        P(None, "lev"),
        P(("lat", "ocn"), "lev"),
        P(("lat", "ocn"), None),
        P(("lat", "ocn"), None),
        P(("lat", "ocn"), None),
    )
    return jax.shard_map(
        body,
        mesh=mesh,
        in_specs=placed,
        out_specs=(
            P(("lat", "ocn"), None, "lev"),
            P(("lat", "ocn"), None),
            P(("lat", "ocn"), None),
            P(("lat", "ocn"), "lev"),
        ),
        check_vma=False,
    )
```

profile of v0, /device:TPU:32, one launch (start us, length us, event | category | flops | bytes accessed | tf_op | source)
XLA Modules:
  0.0 198.1 jit_solution(3094316823144433169)
XLA Ops:
  7.2 0.8 iota_compare_fusion
  8.1 3.6 %broadcast_select_fusion = bf16[2,6,40,5632]{3,2,1,0:T(8,128)(2,1)S(1)} fusion(bf16[2,6,40,5632]{3,2,1,0:T(8,128)(2,1)} %param.9, pred[40,5632]{1,0:T(8,128)(4,1)S(1)} %iota_compare_fusion), kind=kLoop, calls=%fused_computation.16 | loop fusion | flops 2703360 | bytes 11038720 | tf_op jit(solution)/shard_map/jit(_where)/select_n | solution.py:57
  11.7 2.4 %fusion = f32[2,1,40,5632]{3,1,2,0:T(1,128)S(1)} fusion(bf16[2,6,40,5632]{3,2,1,0:T(8,128)(2,1)S(1)} %broadcast_select_fusion, bf16[2,6,1,1]{1,0,2,3:T(2,128)(2,1)S(1)} %bitcast.59), kind=kOutput, calls=%fused_computation.3 | convolution fusion | flops 5406720 | bytes 7208984 | tf_op jit(solution)/shard_map/ql,qljk->qjk/dot_general | solution.py:86
  14.2 1.4 copy.59
  15.6 25.0 %cosine_convert_fusion = (bf16[5632,256]{0,1:T(8,128)(2,1)S(1)}, bf16[5632,256]{0,1:T(8,128)(2,1)S(1)}) fusion(s32[256]{0:T(256)S(1)} %copy-done.8), kind=kLoop, calls=%fused_computation.9 | loop fusion | flops 17301504 | bytes 5768192 | tf_op jit(solution)/shard_map/convert
  40.7 2.9 %pad_maximum_fusion = bf16[5632,512]{0,1:T(8,128)(2,1)} fusion(bf16[5632,256]{0,1:T(8,128)(2,1)S(1)} %get-tuple-element.21, bf16[5632,256]{0,1:T(8,128)(2,1)S(1)} %get-tuple-element.20), kind=kLoop, calls=%fused_computation.7 | loop fusion | flops 11534336 | bytes 11534336 | tf_op jit(solution)/shard_map/concatenate | solution.py:38
  43.6 5.7 %fusion.15 = bf16[256,6,2,2,40]{0,4,3,1,2:T(8,128)(2,1)S(1)} fusion(bf16[2,256,5632,1,1]{2,1,0,4,3:T(8,128)(2,1)} %bitcast.64, bf16[2,6,40,5632]{3,2,1,0:T(8,128)(2,1)S(1)} %bitcast.61, f32[256,40]{0,1:T(8,128)S(1)} %compare_select_fusion), kind=kOutput, calls=%fused_computation.20 | convolution fusion | flops 2768732160 | bytes 11706368 | tf_op jit(solution)/shard_map/dot_general | solution.py:65
  49.4 1.0 copy.32
  50.4 3.4 %reshape.235 = bf16[64,2,1920]{2,1,0:T(2,128)(2,1)} reshape(bf16[256,24,40]{2,1,0:T(8,128)(2,1)S(1)} %copy.32) | data formatting | bytes 983040
  53.8 12.0 %all-to-all-start = ((bf16[64,2,1920]{2,1,0:T(2,128)(2,1)}), bf16[64,2,1920]{2,1,0:T(2,128)(2,1)S(1)}, u32[]{:S(2)}, u32[]{:S(2)}) async-start(bf16[64,2,1920]{2,1,0:T(2,128)(2,1)} %reshape.235), calls=%async_computation | async-start | bytes 983040 | tf_op jit(solution)/shard_map/all_to_all | solution.py:68
  66.6 10.7 %all-reduce.3.cloned.1.call-done = f32[2,40,5632]{2,1,0:T(8,128)} async-done(((f32[2,40,5632]{2,1,0:T(8,128)}), f32[2,40,5632]{2,1,0:T(8,128)}) %all-reduce.3.cloned.1.call-update) | async-done | bytes 1802256 | tf_op jit(solution)/shard_map/psum | solution.py:90
  77.3 1.0 constant_dynamic-slice_fusion
  78.8 3.1 %scatter_custom_fusion = f32[816,256]{1,0:T(8,128)S(1)} fusion(s32[440]{0:T(512)S(1)} %bitcast.81, f32[55,8,2,128]{3,2,1,0:T(2,128)S(1)} %bitcast.75, f32[]{:T(128)} %constant.40.clone.1), kind=kCustom, calls=%fused_computation.35 | custom fusion | flops 112640 | bytes 1286148 | tf_op jit(solution)/shard_map/scatter-add | solution.py:97
  82.0 7.6 %collective-permute-start.3 = (f32[272,256]{1,0:T(8,128)S(1)}, f32[272,256]{1,0:T(8,128)S(1)}, u32[]{:S(2)}, u32[]{:S(2)}) collective-permute-start(f32[272,256]{1,0:T(8,128)S(1)} %get-tuple-element.9), channel_id=1, source_target_pairs={{1,0},{2,1},{3,2},{16,3},{17,16},{18,17},{19,18},{32,19},{33,32},{... | collective-permute-start | bytes 835592 | tf_op jit(solution)/shard_map/ppermute | solution.py:27
  89.6 1.9 collective-permute-start.2
  91.5 7.0 %collective-permute-done.3 = f32[272,256]{1,0:T(8,128)S(1)} collective-permute-done((f32[272,256]{1,0:T(8,128)S(1)}, f32[272,256]{1,0:T(8,128)S(1)}, u32[]{:S(2)}, u32[]{:S(2)}) %collective-permute-start.3) | collective-permute-done | bytes 278560 | tf_op jit(solution)/shard_map/ppermute | solution.py:27
  98.5 10.0 %collective-permute-done.2 = f32[272,256]{1,0:T(8,128)S(1)} collective-permute-done((f32[272,256]{1,0:T(8,128)S(1)}, f32[272,256]{1,0:T(8,128)S(1)}, u32[]{:S(2)}, u32[]{:S(2)}) %collective-permute-start.2) | collective-permute-done | bytes 278560 | tf_op jit(solution)/shard_map/ppermute | solution.py:25
  108.7 0.8 reshape.211
  109.6 1.9 collective-permute-start.1
  111.5 8.8 %collective-permute-start = (f32[2,1,2176]{2,1,0:T(1,128)S(1)}, f32[2,1,2176]{2,1,0:T(1,128)S(1)}, u32[]{:S(2)}, u32[]{:S(2)}) collective-permute-start(f32[2,1,2176]{2,1,0:T(1,128)S(1)} %get-tuple-element.16), channel_id=1, source_target_pairs={{1,0},{2,1},{3,2},{16,3},{17,16},{18,17},{19,18},{32,19},{33,32},{... | collective-permute-start | bytes 52232 | tf_op jit(solution)/shard_map/ppermute | solution.py:27
  120.3 2.5 %reshape.236 = bf16[256,24,40]{2,1,0:T(8,128)(2,1)S(1)} reshape(bf16[64,2,1920]{2,1,0:T(2,128)(2,1)S(1)} %all-to-all-done) | data formatting | bytes 983040
  123.5 3.9 %all_to_all.16 = bf16[4,24,2560]{2,1,0:T(8,128)(2,1)} reshape(bf16[4,24,64,40]{3,2,1,0:T(8,128)(2,1)S(1)} %copy.33) | data formatting | bytes 983040 | tf_op jit(solution)/shard_map/all_to_all | solution.py:68
  127.8 22.7 %all-reduce.5.cloned.1.call-done = f32[2,16,2176]{2,1,0:T(8,128)} async-done(((f32[2,16,2176]{2,1,0:T(8,128)}), f32[2,16,2176]{2,1,0:T(8,128)}) %all-reduce.5.cloned.1.call-update) | async-done | bytes 278544 | tf_op jit(solution)/shard_map/psum | solution.py:102
  150.5 1.2 fusion.31
  152.3 5.4 %collective-permute-start.5 = (f32[16,2176]{1,0:T(8,128)S(1)}, f32[16,2176]{1,0:T(8,128)S(1)}, u32[]{:S(2)}, u32[]{:S(2)}) collective-permute-start(f32[16,2176]{1,0:T(8,128)S(1)} %get-tuple-element.11), channel_id=1, source_target_pairs={{1,0},{2,1},{3,2},{16,3},{17,16},{18,17},{19,18},{32,19},{33,32},{... | collective-permute-start | bytes 417800 | tf_op jit(solution)/shard_map/ppermute | solution.py:27
  157.7 1.9 collective-permute-start.4
  159.8 1.5 collective-permute-done.5
  161.3 10.8 %collective-permute-done.4 = f32[16,2176]{1,0:T(8,128)S(1)} collective-permute-done((f32[16,2176]{1,0:T(8,128)S(1)}, f32[16,2176]{1,0:T(8,128)S(1)}, u32[]{:S(2)}, u32[]{:S(2)}) %collective-permute-start.4) | collective-permute-done | bytes 139296 | tf_op jit(solution)/shard_map/ppermute | solution.py:25
  172.1 1.2 gather_fusion
  173.5 0.8 select_select_fusion
  174.3 11.3 %all-gather.2.cloned.1.call-done = bf16[4,96,2560]{2,1,0:T(8,128)(2,1)} async-done(((bf16[4,24,2560]{2,1,0:T(8,128)(2,1)}), bf16[4,96,2560]{2,1,0:T(8,128)(2,1)}) %all-gather.2.cloned.1.call-update) | async-done | bytes 1966096 | tf_op jit(solution)/shard_map/all_gather | solution.py:77
  185.5 6.1 %fusion.44 = f32[4,96,384]{2,1,0:T(8,128)} fusion(bf16[4,96,2560]{2,1,0:T(8,128)(2,1)} %all-gather.2.cloned.1.call-done, bf16[4,2560,384]{2,1,0:T(8,128)(2,1)} %param.12), kind=kOutput, calls=%fused_computation.87 | convolution fusion | flops 754974720 | bytes 10420224 | tf_op jit(solution)/shard_map/srj,sjd->srd/dot_general | solution.py:75
  (66 shorter events, 3.8 us)
Async XLA Ops:
  7.2 4.5 %copy-start = (bf16[2,6]{1,0:T(2,128)(2,1)S(1)}, bf16[2,6]{1,0:T(2,128)(2,1)}, u32[]{:S(2)}) copy-start(bf16[2,6]{1,0:T(2,128)(2,1)} %param.13) | copy-start | bytes 76
  7.2 70.1 %all-reduce.3.cloned.1.call-start = ((), (), s32[]{:S(2)}) async-start(), calls=%async_computation.2 | async-start | bytes 3604480 | tf_op jit(solution)/shard_map/psum | solution.py:90
  11.7 3.8 %copy-start.1 = (bf16[2,6,40,5632]{3,2,1,0:T(8,128)(2,1)}, bf16[2,6,40,5632]{3,2,1,0:T(8,128)(2,1)S(1)}, u32[]{:S(2)}) copy-start(bf16[2,6,40,5632]{3,2,1,0:T(8,128)(2,1)S(1)} %broadcast_select_fusion) | copy-start | bytes 16220164
  11.7 3.8 %copy-start.7 = (s32[40]{0:T(128)S(1)}, s32[40]{0:T(128)}, u32[]{:S(2)}) copy-start(s32[40]{0:T(128)} %param.10) | copy-start | bytes 484
  11.7 3.8 %copy-start.8 = (s32[256]{0:T(256)S(1)}, s32[256]{0:T(256)}, u32[]{:S(2)}) copy-start(s32[256]{0:T(256)} %param.11) | copy-start | bytes 3076
  15.6 28.0 %slice-start = ((s8[5406720]{0:T(1024)(128)(4,1)}), s8[4194304]{0:T(1024)(128)(4,1)S(1)}, s32[]{:S(2)}) async-start(s8[5406720]{0:T(1024)(128)(4,1)} %bitcast.60), calls=%async_computation.4 | async-start | bytes 8388608
  40.6 3.0 %slice-start.1 = ((s8[5406720]{0:T(1024)(128)(4,1)}), s8[1212416]{0:T(1024)(128)(4,1)S(1)}, s32[]{:S(2)}) async-start(s8[5406720]{0:T(1024)(128)(4,1)} %bitcast.60), calls=%async_computation.5 | async-start | bytes 2424832
  49.3 16.5 %copy-start.5 = (s32[40,11]{0,1:T(8,128)S(1)}, s32[40,11]{0,1:T(8,128)}, u32[]{:S(2)}) copy-start(s32[40,11]{0,1:T(8,128)} %param.14) | copy-start | bytes 5284
  53.8 55.8 %copy-start.2 = (f32[16,2176]{1,0:T(8,128)S(1)}, f32[16,2176]{1,0:T(8,128)}, u32[]{:S(2)}) copy-start(f32[16,2176]{1,0:T(8,128)} %param.15) | copy-start | bytes 417796
  53.8 55.8 %copy-start.3 = (f32[16,2176]{1,0:T(8,128)S(1)}, f32[16,2176]{1,0:T(8,128)}, u32[]{:S(2)}) copy-start(f32[16,2176]{1,0:T(8,128)} %param.16) | copy-start | bytes 417796
  53.8 66.5 %all-to-all-start = ((bf16[64,2,1920]{2,1,0:T(2,128)(2,1)}), bf16[64,2,1920]{2,1,0:T(2,128)(2,1)S(1)}, u32[]{:S(2)}, u32[]{:S(2)}) async-start(bf16[64,2,1920]{2,1,0:T(2,128)(2,1)} %reshape.235), calls=%async_computation | async-start | bytes 983040 | tf_op jit(solution)/shard_map/all_to_all | solution.py:68
  65.8 84.7 %all-reduce.5.cloned.1.call-start = ((), (), s32[]{:S(2)}) async-start(), calls=%async_computation.3 | async-start | bytes 557056 | tf_op jit(solution)/shard_map/psum | solution.py:102
  82.0 16.5 %collective-permute-start.3 = (f32[272,256]{1,0:T(8,128)S(1)}, f32[272,256]{1,0:T(8,128)S(1)}, u32[]{:S(2)}, u32[]{:S(2)}) collective-permute-start(f32[272,256]{1,0:T(8,128)S(1)} %get-tuple-element.9), channel_id=1, source_target_pairs={{1,0},{2,1},{3,2},{16,3},{17,16},{18,17},{19,18},{32,19},{33,32},{... | collective-permute-start | bytes 835592 | tf_op jit(solution)/shard_map/ppermute | solution.py:27
  89.6 18.9 %collective-permute-start.2 = (f32[272,256]{1,0:T(8,128)S(1)}, f32[272,256]{1,0:T(8,128)S(1)}, u32[]{:S(2)}, u32[]{:S(2)}) collective-permute-start(f32[272,256]{1,0:T(8,128)S(1)} %get-tuple-element.8), channel_id=1, source_target_pairs={{0,1},{1,2},{2,3},{3,16},{16,17},{17,18},{18,19},{19,32},{32,33},{... | collective-permute-start | bytes 835592 | tf_op jit(solution)/shard_map/ppermute | solution.py:25
  108.5 18.8 %copy-start.6 = (s32[16,17]{1,0:T(8,128)S(1)}, s32[16,17]{1,0:T(8,128)}, u32[]{:S(2)}) copy-start(s32[16,17]{1,0:T(8,128)} %param.17) | copy-start | bytes 3268
  109.5 76.0 %all-gather.2.cloned.1.call-start = ((), (), s32[]{:S(2)}) async-start(), calls=%async_computation.1 | async-start | bytes 2457600 | tf_op jit(solution)/shard_map/all_gather | solution.py:77
  109.6 18.1 %collective-permute-start.1 = (f32[2,1,2176]{2,1,0:T(1,128)S(1)}, f32[2,1,2176]{2,1,0:T(1,128)S(1)}, u32[]{:S(2)}, u32[]{:S(2)}) collective-permute-start(f32[2,1,2176]{2,1,0:T(1,128)S(1)} %get-tuple-element.17), channel_id=1, source_target_pairs={{0,1},{1,2},{2,3},{3,16},{16,17},{17,18},{18,19},{19,32},{32,33},{... | collective-permute-start | bytes 52232 | tf_op jit(solution)/shard_map/ppermute | solution.py:25
  111.5 16.2 %collective-permute-start = (f32[2,1,2176]{2,1,0:T(1,128)S(1)}, f32[2,1,2176]{2,1,0:T(1,128)S(1)}, u32[]{:S(2)}, u32[]{:S(2)}) collective-permute-start(f32[2,1,2176]{2,1,0:T(1,128)S(1)} %get-tuple-element.16), channel_id=1, source_target_pairs={{1,0},{2,1},{3,2},{16,3},{17,16},{18,17},{19,18},{32,19},{33,32},{... | collective-permute-start | bytes 52232 | tf_op jit(solution)/shard_map/ppermute | solution.py:27
  152.3 39.3 %copy-start.4 = (f32[16,2176]{1,0:T(8,128)}, f32[16,2176]{1,0:T(8,128)S(1)}, u32[]{:S(2)}) copy-start(f32[16,2176]{1,0:T(8,128)S(1)} %get-tuple-element.11) | copy-start | bytes 417796
  152.3 9.0 %collective-permute-start.5 = (f32[16,2176]{1,0:T(8,128)S(1)}, f32[16,2176]{1,0:T(8,128)S(1)}, u32[]{:S(2)}, u32[]{:S(2)}) collective-permute-start(f32[16,2176]{1,0:T(8,128)S(1)} %get-tuple-element.11), channel_id=1, source_target_pairs={{1,0},{2,1},{3,2},{16,3},{17,16},{18,17},{19,18},{32,19},{33,32},{... | collective-permute-start | bytes 417800 | tf_op jit(solution)/shard_map/ppermute | solution.py:27
  157.7 14.3 %collective-permute-start.4 = (f32[16,2176]{1,0:T(8,128)S(1)}, f32[16,2176]{1,0:T(8,128)S(1)}, u32[]{:S(2)}, u32[]{:S(2)}) collective-permute-start(f32[16,2176]{1,0:T(8,128)S(1)} %get-tuple-element.11), channel_id=1, source_target_pairs={{0,1},{1,2},{2,3},{3,16},{16,17},{17,18},{18,19},{19,32},{32,33},{... | collective-permute-start | bytes 417800 | tf_op jit(solution)/shard_map/ppermute | solution.py:25
Sparse Core Ops, SparseCore 0:
  15.7 61.5 all-reduce.2
  109.6 40.7 all-reduce.4
  153.0 32.5 all-gather.1
where the time goes:
time: 200 us; the launch traced here: 198 us
  waiting for transfers between devices  74 us (37%)
  starting transfers between devices  39.6 us (20%)
  other arithmetic  37.9 us (19%)
  local copies, waits for them, and re-layouts  18.2 us (9%)
  matrix products  14.2 us (7%)
  between operations  14.2 us (7%)
    another operation x1, other arithmetic  25 us
    psum x1, waiting for transfers between devices, body(): tile_sums = lax.psum(arrived, 'lev')  22.7 us
    ppermute x3, starting transfers between devices, with_halo(): lax.ppermute(head, axis, [((i + 1) % count, i) for i in range(ends)])  21.7 us
    ppermute x3, waiting for transfers between devices, with_halo(): lax.ppermute(tail, axis, [(i, (i + 1) % count) for i in range(ends)])  20.8 us
    all_to_all x1, starting transfers between devices, body(): lax.all_to_all(coeffs.transpose(4, 1, 0, 3, 2).reshape(wave_count, lev_de...  12 us
    all_gather x1, waiting for transfers between devices, body(): lax.all_gather(regrouped, 'lev', axis=1, tiled=True)  11.3 us
    psum x1, waiting for transfers between devices, body(): totals = lax.psum(partial_sum, 'lev')  10.7 us
    ppermute x3, waiting for transfers between devices, with_halo(): lax.ppermute(head, axis, [((i + 1) % count, i) for i in range(ends)])  8.47 us
  transfers between devices with their start and end apart: 10, of which 7 were waited for; matrix products, arithmetic and copies ran while one was open for 26% of the time, Pallas kernels for 0%

commit v1 on v0

v1 whole, which is shorter than its diff:
```python
import math

import jax
import jax.numpy as jnp
from jax import lax
from jax.experimental import pallas as pl
from jax.experimental.pallas import tpu as pltpu
from jax.sharding import PartitionSpec as P

BLOCK = 128
FULL_TURN = 2.0 * math.pi
DIFFUSION = 0.2
COUPLING = 0.5
CHUNK = 512


def local_kernel(
    x_ref, lat_ref, wcol_ref, root_ref, slot_ref, fine1_ref, fine2_ref, coarse1_ref, coarse2_ref,
    msg_ref, tiles_ref, masked, table, acc, blocks_hi, blocks_lo,
):
    step = pl.program_id(0)
    pair_rows = lat_ref.shape[0]
    pairs = x_ref.shape[0] // pair_rows
    band = pair_rows // 2
    width = x_ref.shape[1]
    blocks = width // BLOCK

    for a in range(blocks):
        row1 = coarse1_ref[0, a : a + 1, :]
        row2 = coarse2_ref[0, a : a + 1, :]
        table[a * BLOCK : (a + 1) * BLOCK, :] = (
            fine1_ref[...] * row1 + fine2_ref[...] * row2
        ).astype(jnp.bfloat16)

    points = step * width + lax.broadcasted_iota(jnp.int32, (pair_rows, width), 1)
    keep = points < lat_ref[...]
    for f in range(2):
        total = None
        for p in range(pairs // 2):
            rows = slice((f * (pairs // 2) + p) * pair_rows, (f * (pairs // 2) + p + 1) * pair_rows)
            part = jnp.where(keep, x_ref[rows, :].astype(jnp.float32), 0.0)
            masked[rows, :] = part.astype(jnp.bfloat16)
            term = part * wcol_ref[rows, :]
            total = term if total is None else total + term
        flux = total[:band] + total[band:]
        for two in range(blocks // 2):
            pair = jnp.concatenate(
                [flux[:, (2 * two) * BLOCK : (2 * two + 1) * BLOCK], flux[:, (2 * two + 1) * BLOCK : (2 * two + 2) * BLOCK]],
                axis=0,
            )
            high = pair.astype(jnp.bfloat16)
            low = (pair - high.astype(jnp.float32)).astype(jnp.bfloat16)
            start = pl.multiple_of((step * (blocks // 2) + two) * pair_rows, 16)
            blocks_hi[pl.ds(start, pair_rows), f * BLOCK : (f + 1) * BLOCK] = high
            blocks_lo[pl.ds(start, pair_rows), f * BLOCK : (f + 1) * BLOCK] = low

    rows = x_ref.shape[0]
    product = jnp.dot(masked[...], table[...], preferred_element_type=jnp.float32)

    @pl.when(step == 0)
    def _():
        acc[:rows, :] = product
        acc[rows:, :] = jnp.zeros((acc.shape[0] - rows, acc.shape[1]), jnp.float32)

    @pl.when(step > 0)
    def _():
        acc[:rows, :] += product

    @pl.when(step == pl.num_programs(0) - 1)
    def _():
        for p in range(pairs):
            acc[p * pair_rows : (p + 1) * pair_rows, :] *= root_ref[...]
        turned = acc[...].T.astype(jnp.bfloat16)
        msg_ref[...] = turned.reshape(msg_ref.shape)
        part_rows = tiles_ref.shape[2]
        for sec in range(3):
            for h in range(2):
                base = (sec * 2 + h) * part_rows
                ids = base + lax.broadcasted_iota(jnp.int32, (part_rows, slot_ref.shape[1]), 0)
                hot = jnp.where(slot_ref[...] == ids, 1.0, 0.0).astype(jnp.bfloat16)
                sums = jnp.dot(hot, blocks_hi[...], preferred_element_type=jnp.float32)
                sums += jnp.dot(hot, blocks_lo[...], preferred_element_type=jnp.float32)
                for f in range(2):
                    tiles_ref[sec, f * 2 + h] = sums[:, f * BLOCK : (f + 1) * BLOCK].astype(tiles_ref.dtype)


def local_part(fields, lat_points, wave_order, column_weight, slots, groups):
    nf, nl, band, length = fields.shape
    rows = nf * nl * band
    waves = wave_order.shape[0]
    each = waves // groups
    cols = 2 * waves
    order = jnp.broadcast_to(wave_order.reshape(groups, 1, each), (groups, 2, each)).reshape(1, cols)
    imag = (lax.broadcasted_iota(jnp.int32, (1, cols), 1) // each) % 2 == 1
    unit = FULL_TURN / length
    fine = (order * jnp.arange(BLOCK, dtype=jnp.int32)[:, None] % length).astype(jnp.float32) * unit
    coarse = (
        order * (BLOCK * jnp.arange(length // BLOCK, dtype=jnp.int32)[:, None]) % length
    ).astype(jnp.float32) * unit
    fc, fs = jnp.cos(fine), jnp.sin(fine)
    cc, cs = jnp.cos(coarse), jnp.sin(coarse)
    fine1, fine2 = jnp.where(imag, fs, fc), jnp.where(imag, fc, fs)
    coarse1, coarse2 = jnp.where(imag, -cc, cc), -cs
    steps = length // CHUNK
    coarse1 = coarse1.reshape(steps, CHUNK // BLOCK, cols)
    coarse2 = coarse2.reshape(steps, CHUNK // BLOCK, cols)
    inverse_root = 1.0 / jnp.sqrt(lat_points.astype(jnp.float32))
    root = jnp.where(2 * order < lat_points[:, None], inverse_root[:, None], 0.0)
    root = jnp.concatenate([root, root], axis=0)
    lat2 = jnp.concatenate([lat_points, lat_points])[:, None]
    wcol = jnp.broadcast_to(column_weight.astype(jnp.float32)[:, :, None], (nf, nl, band)).reshape(rows, 1)
    slot_row = slots.T.reshape(1, -1)
    whole = lambda shape: pl.BlockSpec(shape, lambda i: (0,) * len(shape))
    lanes = 512
    tile_parts = (3, 4, 136, BLOCK)
    return pl.pallas_call(
        local_kernel,
        grid=(steps,),
        in_specs=[
            pl.BlockSpec((rows, CHUNK), lambda i: (0, i)),
            whole(lat2.shape),
            whole(wcol.shape),
            whole(root.shape),
            whole(slot_row.shape),
            whole(fine1.shape),
            whole(fine2.shape),
            pl.BlockSpec((1, CHUNK // BLOCK, cols), lambda i: (i, 0, 0)),
            pl.BlockSpec((1, CHUNK // BLOCK, cols), lambda i: (i, 0, 0)),
        ],
        out_specs=[whole((groups, 2 * each, lanes)), whole(tile_parts)],
        out_shape=[
            jax.ShapeDtypeStruct((groups, 2 * each, lanes), jnp.bfloat16),
            jax.ShapeDtypeStruct(tile_parts, jnp.float32),
        ],
        scratch_shapes=[
            pltpu.VMEM((rows, CHUNK), jnp.bfloat16),
            pltpu.VMEM((CHUNK, cols), jnp.bfloat16),
            pltpu.VMEM((lanes, cols), jnp.float32),
            pltpu.VMEM((slot_row.shape[1], 2 * BLOCK), jnp.bfloat16),
            pltpu.VMEM((slot_row.shape[1], 2 * BLOCK), jnp.bfloat16),
        ],
        compiler_params=pltpu.CompilerParams(vmem_limit_bytes=48 * 1024 * 1024),
    )(fields.reshape(rows, length), lat2, wcol, root, slot_row, fine1, fine2, coarse1, coarse2)


def ring_gather(piece, axis):
    count = lax.axis_size(axis)
    me = lax.axis_index(axis)
    pieces = [piece]
    for hop in range(1, count):
        pieces.append(lax.ppermute(piece, axis, [(i, (i + hop) % count) for i in range(count)]))
    twice = jnp.stack(pieces[::-1] + pieces[::-1])
    return lax.dynamic_slice_in_dim(twice, count - 1 - me, count, 0)


def body(
    atmos_fields,
    lat_points,
    wave_order,
    legendre,
    column_weight,
    block_remap,
    ocean_temp,
    ocean_salt,
    sea_mask,
):
    both = ("lat", "ocn")
    nf, nl, band, length = atmos_fields.shape
    groups = lax.axis_size(both)
    levs = lax.axis_size("lev")
    g = lax.axis_index(both)
    orow, ocols = ocean_temp.shape
    tcols = ocols // BLOCK
    tile_count = orow * tcols

    def slot_of(targets):
        local = targets - (g - 1) * tile_count
        sec, inside = local // tile_count, local % tile_count
        r, c = inside // tcols, inside % tcols
        return sec * tile_count + (r // 8) * (tcols * 8) + c * 8 + r % 8

    remap = ring_gather(block_remap, "lev").transpose(1, 0, 2).reshape(band, -1)
    msg, parts = local_part(
        atmos_fields, lat_points, wave_order, column_weight, slot_of(remap), groups
    )
    got = lax.all_to_all(msg, both, split_axis=0, concat_axis=0, tiled=True)
    each = wave_order.shape[0] // groups
    own = got[:, :, : nf * nl * band].reshape(groups, 2, each, nf, nl, band)
    own = own.transpose(2, 4, 3, 1, 0, 5).reshape(each, nl * nf * 2, groups * band)
    coeffs = ring_gather(own, "lev").transpose(1, 0, 2, 3).reshape(each, levs * nl * nf * 2, groups * band)
    spectra = jnp.einsum("srj,sjd->srd", coeffs, legendre, preferred_element_type=jnp.float32)

    up = [(i, (i + 1) % groups) for i in range(groups)]
    down = [((i + 1) % groups, i) for i in range(groups)]
    arrived = parts[1] + lax.ppermute(parts[2], both, up) + lax.ppermute(parts[0], both, down)
    sums = jnp.sum(lax.all_to_all(arrived, "lev", split_axis=0, concat_axis=0, tiled=True).reshape(levs, -1, BLOCK), 0)
    sums = ring_gather(sums, "lev")
    forcing = (
        sums.reshape(2, orow // 8, tcols, 8, BLOCK).transpose(0, 1, 3, 2, 4).reshape(2, orow, ocols)
    )
    sea = jnp.broadcast_to(sea_mask[:, :, None], (orow, tcols, BLOCK)).reshape(orow, ocols).astype(jnp.float32)
    state = jnp.stack([ocean_temp, ocean_salt])
    above = lax.ppermute(state[:, -1:], both, up[:-1])
    below = lax.ppermute(state[:, :1], both, down[:-1])
    padded = jnp.concatenate([above, state, below], axis=1)
    laplace = (
        padded[:, 2:] + padded[:, :-2] + jnp.roll(state, 1, 2) + jnp.roll(state, -1, 2) - 4.0 * state
    )
    updated = state + DIFFUSION * laplace + COUPLING * sea[None] * forcing
    temp_next, salt_next = updated[0], updated[1]
    near = jnp.concatenate(
        [lax.ppermute(temp_next, both, up), temp_next, lax.ppermute(temp_next, both, down)], axis=0
    ).reshape(3 * tile_count, BLOCK)
    local = block_remap.reshape(-1) - (g - 1) * tile_count
    quarter = length // levs
    surface = jnp.take(near, local, axis=0).reshape(band, quarter)
    own_points = lax.axis_index("lev") * quarter + jnp.arange(quarter, dtype=jnp.int32)
    surface_temp = jnp.where(own_points[None, :] < lat_points[:, None], surface, 0.0)
    return (spectra, temp_next, salt_next, surface_temp)


def solution(mesh):
    both = ("lat", "ocn")
    placed = (
        P(None, "lev", both, None),
        P(both),
        P(),
        P(both, None, "lev"),
        P(None, "lev"),
        P(both, "lev"),
        P(both, None),
        P(both, None),
        P(both, None),
    )
    return jax.shard_map(
        body,
        mesh=mesh,
        in_specs=placed,
        out_specs=(P(both, None, "lev"), P(both, None), P(both, None), P(both, "lev")),
        check_vma=False,
    )
```

time: 200 us -> 140 us (0.70)
  other arithmetic: 37.9 us -> 8.65 us
  waiting for transfers between devices: 74 us -> 48.4 us
  Pallas kernels: 0 us -> 13.3 us
  between operations: 14.2 us -> 1.13 us
  matrix products: 14.2 us -> 2.24 us
  starting transfers between devices: 39.6 us -> 47.4 us
    psum x2 -> x0, waiting for transfers between devices: 33.4 us -> none  [the longest x1 22.7 us: body(): tile_sums = lax.psum(arrived, 'lev')]
    another operation x4 -> x3, other arithmetic: 25.3 us -> 1.22 us  [body(): state = jnp.stack([ocean_temp, ocean_salt])]
    all_to_all x1 -> x2, waiting for transfers between devices: 0.01 us -> 13.4 us  [the longest x1 6.72 us: body(): lax.all_to_all(arrived, 'lev', split_axis=0, concat_axis=0, tiled=True)]
    pallas_call x0 -> x1, Pallas kernels: none -> 13.3 us  [local_part(): pl.pallas_call(local_kernel, grid=(steps,), in_specs=[pl.BlockSpec((rows,...]
    dot_general x3 -> x1, matrix products: 14.2 us -> 2.24 us  [body(): jnp.einsum('srj,sjd->srd', coeffs, legendre, preferred_element_type=jnp.f...]
    all_gather x1 -> x0, waiting for transfers between devices: 11.3 us -> none  [body(): lax.all_gather(regrouped, 'lev', axis=1, tiled=True)]
    ppermute x6 -> x15, starting transfers between devices: 27.5 us -> 34.7 us  [the longest x9 12.9 us: ring_gather(): lax.ppermute(piece, axis, [(i, (i + hop) % count) for i in range(count)])]
    ppermute x6 -> x15, waiting for transfers between devices: 29.2 us -> 35 us  [the longest x9 26.2 us: ring_gather(): lax.ppermute(piece, axis, [(i, (i + hop) % count) for i in range(count)])]
  transfers between devices with their start and end apart: 10 -> 17, of which waited for: 7 -> 7; matrix products, arithmetic and copies ran while one was open for 26% -> 17% of each run, Pallas kernels for 0% -> 10%
where the time goes in v1:
time: 140 us; the launch traced here: 139 us
  waiting for transfers between devices  48.4 us (35%)
  starting transfers between devices  47.4 us (34%)
  local copies, waits for them, and re-layouts  17.7 us (13%)
  Pallas kernels  13.3 us (10%)
  other arithmetic  8.65 us (6%)
  matrix products  2.24 us (2%)
    ppermute x9, waiting for transfers between devices, ring_gather(): lax.ppermute(piece, axis, [(i, (i + hop) % count) for i in range(count)])  26.2 us
    pallas_call x1, Pallas kernels, local_part(): pl.pallas_call(local_kernel, grid=(steps,), in_specs=[pl.BlockSpec((rows,...  13.3 us
    ppermute x9, starting transfers between devices, ring_gather(): lax.ppermute(piece, axis, [(i, (i + hop) % count) for i in range(count)])  12.9 us
    all_to_all x1, starting transfers between devices, body(): got = lax.all_to_all(msg, both, split_axis=0, concat_axis=0, tiled=True)  9.33 us
    ppermute x1, starting transfers between devices, body(): below = lax.ppermute(state[:, :1], both, down[:-1])  8.8 us
    ppermute x1, waiting for transfers between devices, body(): lax.ppermute(parts[2], both, up)  8.79 us
    all_to_all x1, waiting for transfers between devices, body(): lax.all_to_all(arrived, 'lev', split_axis=0, concat_axis=0, tiled=True)  6.72 us
    all_to_all x1, waiting for transfers between devices, body(): got = lax.all_to_all(msg, both, split_axis=0, concat_axis=0, tiled=True)  6.72 us
  transfers between devices with their start and end apart: 17, of which 7 were waited for; matrix products, arithmetic and copies ran while one was open for 17% of the time, Pallas kernels for 10%

profile of v1, /device:TPU:32, one launch (start us, length us, event | category | flops | bytes accessed | tf_op | source)
XLA Modules:
  0.0 139.0 jit_solution(7503243186849500018)
XLA Ops:
  0.6 1.6 %collective-permute-start.2 = (s32[40,11]{0,1:T(8,128)}, s32[40,11]{0,1:T(8,128)S(1)}, u32[]{:S(2)}, u32[]{:S(2)}) collective-permute-start(s32[40,11]{0,1:T(8,128)} %param.14), channel_id=1, source_target_pairs={{0,4},{4,8},{8,12},{12,0},{1,5},{5,9},{9,13},{13,1},{2,6},{6,10},{... | collective-permute-start | bytes 5288 | tf_op jit(solution)/shard_map/ppermute | solution.py:151
  2.2 2.7 %collective-permute-start.1 = (s32[40,11]{0,1:T(8,128)}, s32[40,11]{0,1:T(8,128)S(1)}, u32[]{:S(2)}, u32[]{:S(2)}) collective-permute-start(s32[40,11]{0,1:T(8,128)} %param.14), channel_id=1, source_target_pairs={{0,8},{4,12},{8,0},{12,4},{1,9},{5,13},{9,1},{13,5},{2,10},{6,14},... | collective-permute-start | bytes 5288 | tf_op jit(solution)/shard_map/ppermute | solution.py:151
  4.9 1.4 %collective-permute-start = (s32[40,11]{0,1:T(8,128)}, s32[40,11]{0,1:T(8,128)S(1)}, u32[]{:S(2)}, u32[]{:S(2)}) collective-permute-start(s32[40,11]{0,1:T(8,128)} %param.14), channel_id=1, source_target_pairs={{0,12},{4,0},{8,4},{12,8},{1,13},{5,1},{9,5},{13,9},{2,14},{6,2},{... | collective-permute-start | bytes 5288 | tf_op jit(solution)/shard_map/ppermute | solution.py:151
  6.4 1.0 fusion.37
  7.4 8.8 %collective-permute-start.6 = (f32[2,1,2176]{2,1,0:T(1,128)S(1)}, f32[2,1,2176]{2,1,0:T(1,128)S(1)}, u32[]{:S(2)}, u32[]{:S(2)}) collective-permute-start(f32[2,1,2176]{2,1,0:T(1,128)S(1)} %get-tuple-element.18), channel_id=1, source_target_pairs={{1,0},{2,1},{3,2},{16,3},{17,16},{18,17},{19,18},{32,19},{33,32},{... | collective-permute-start | bytes 52232 | tf_op jit(solution)/shard_map/ppermute | solution.py:204
  16.2 1.9 %collective-permute-start.7 = (f32[2,1,2176]{2,1,0:T(1,128)S(1)}, f32[2,1,2176]{2,1,0:T(1,128)S(1)}, u32[]{:S(2)}, u32[]{:S(2)}) collective-permute-start(f32[2,1,2176]{2,1,0:T(1,128)S(1)} %get-tuple-element.19), channel_id=1, source_target_pairs={{0,1},{1,2},{2,3},{3,16},{16,17},{17,18},{18,19},{19,32},{32,33},{... | collective-permute-start | bytes 52232 | tf_op jit(solution)/shard_map/ppermute | solution.py:203
  21.9 1.1 fusion.16
  23.0 0.8 sine_negate_fusion
  23.9 0.8 add_bitcast_fusion
  27.8 13.3 %shard_map.120 = (bf16[64,8,512]{2,1,0:T(8,128)(2,1)}, f32[3,4,136,128]{3,2,1,0:T(8,128)S(1)}) custom-call(bf16[480,5632]{1,0:T(8,128)(2,1)} %bitcast.93, s32[80,1]{1,0:T(8,128)S(1)} %copy.19.lat_ref, f32[480,1]{1,0:T(8,128)S(1)} %reshape.215.wcol_ref, f32[80,512]{1,0:T(8,128)S(1)} %pad_maximum_fusion.6.root_ref, s32[1,1760]{1,0:T(1,128)S(1)} %reshape.200.slot_ref, ...), custom_call_target="tpu_custom_call" | custom-call | tf_op jit(solution)/shard_map/pallas_call | solution.py:116
  41.7 6.5 %collective-permute-start.9 = (f32[4,136,128]{2,1,0:T(8,128)S(1)}, f32[4,136,128]{2,1,0:T(8,128)S(1)}, u32[]{:S(2)}, u32[]{:S(2)}) collective-permute-start(f32[4,136,128]{2,1,0:T(8,128)S(1)} %get-tuple-element.11), channel_id=1, source_target_pairs={{1,0},{2,1},{3,2},{16,3},{17,16},{18,17},{19,18},{32,19},{33,32},{... | collective-permute-start | bytes 835592 | tf_op jit(solution)/shard_map/ppermute | solution.py:195
  48.3 8.8 %collective-permute-done.8 = f32[4,136,128]{2,1,0:T(8,128)S(1)} collective-permute-done((f32[4,136,128]{2,1,0:T(8,128)S(1)}, f32[4,136,128]{2,1,0:T(8,128)S(1)}, u32[]{:S(2)}, u32[]{:S(2)}) %collective-permute-start.8) | collective-permute-done | bytes 278560 | tf_op jit(solution)/shard_map/ppermute | solution.py:195
  57.9 3.4 %all-to-all-start.1 = ((f32[4,136,128]{2,1,0:T(8,128)}), f32[4,136,128]{2,1,0:T(8,128)S(1)}, u32[]{:S(2)}, u32[]{:S(2)}) async-start(f32[4,136,128]{2,1,0:T(8,128)} %fusion.9), calls=%async_computation.1 | async-start | bytes 557056 | tf_op jit(solution)/shard_map/all_to_all | solution.py:196
  61.3 6.7 %all-to-all-done.1 = f32[4,136,128]{2,1,0:T(8,128)S(1)} async-done(((f32[4,136,128]{2,1,0:T(8,128)}), f32[4,136,128]{2,1,0:T(8,128)S(1)}, u32[]{:S(2)}, u32[]{:S(2)}) %all-to-all-start.1) | async-done | bytes 278560 | tf_op jit(solution)/shard_map/all_to_all | solution.py:196
  68.1 1.2 collective-permute-start.10
  69.4 9.3 %all-to-all-start = ((bf16[64,8,512]{2,1,0:T(8,128)(2,1)}), bf16[64,8,512]{2,1,0:T(8,128)(2,1)S(1)}, u32[]{:S(2)}, u32[]{:S(2)}) async-start(bf16[64,8,512]{2,1,0:T(8,128)(2,1)} %get-tuple-element.6), calls=%async_computation | async-start | bytes 1048576 | tf_op jit(solution)/shard_map/all_to_all | solution.py:186
  78.7 0.9 collective-permute-start.12
  79.7 1.1 collective-permute-start.11
  80.7 4.8 %collective-permute-done.11 = f32[136,128]{1,0:T(8,128)S(1)} collective-permute-done((f32[136,128]{1,0:T(8,128)S(1)}, f32[136,128]{1,0:T(8,128)S(1)}, u32[]{:S(2)}, u32[]{:S(2)}) %collective-permute-start.11) | collective-permute-done | bytes 69664 | tf_op jit(solution)/shard_map/ppermute | solution.py:151
  86.8 4.0 %collective-permute-start.14 = (f32[16,2176]{1,0:T(8,128)S(1)}, f32[16,2176]{1,0:T(8,128)S(1)}, u32[]{:S(2)}, u32[]{:S(2)}) collective-permute-start(f32[16,2176]{1,0:T(8,128)S(1)} %get-tuple-element.13), channel_id=1, source_target_pairs={{1,0},{2,1},{3,2},{16,3},{17,16},{18,17},{19,18},{32,19},{33,32},{... | collective-permute-start | bytes 417800 | tf_op jit(solution)/shard_map/ppermute | solution.py:212
  90.9 6.7 %all-to-all-done = bf16[64,8,512]{2,1,0:T(8,128)(2,1)S(1)} async-done(((bf16[64,8,512]{2,1,0:T(8,128)(2,1)}), bf16[64,8,512]{2,1,0:T(8,128)(2,1)S(1)}, u32[]{:S(2)}, u32[]{:S(2)}) %all-to-all-start) | async-done | bytes 524320 | tf_op jit(solution)/shard_map/all_to_all | solution.py:186
  98.3 0.9 copy.22
  99.2 3.8 %reshape.202 = bf16[4,24,2560]{2,1,0:T(8,128)(2,1)} reshape(bf16[4,6,2,2,64,40]{5,4,3,2,1,0:T(8,128)(2,1)S(1)} %copy.22) | data formatting | bytes 983040 | tf_op jit(solution)/shard_map/reshape | solution.py:189
  103.2 1.2 gather_fusion
  105.4 3.0 %stack_reshape.4 = bf16[1,4,24,2560]{3,2,1,0:T(8,128)(2,1)S(1)} reshape(bf16[4,6,2,2,64,40]{5,4,3,2,1,0:T(8,128)(2,1)S(1)} %copy.22) | data formatting | bytes 983040 | tf_op jit(solution)/shard_map/stack;reshape | solution.py:152
  108.4 1.9 %collective-permute-start.5 = (bf16[4,24,2560]{2,1,0:T(8,128)(2,1)}, bf16[4,24,2560]{2,1,0:T(8,128)(2,1)S(1)}, u32[]{:S(2)}, u32[]{:S(2)}) collective-permute-start(bf16[4,24,2560]{2,1,0:T(8,128)(2,1)} %reshape.202), channel_id=1, source_target_pairs={{0,4},{4,8},{8,12},{12,0},{1,5},{5,9},{9,13},{13,1},{2,6},{6,10},{... | collective-permute-start | bytes 1474568 | tf_op jit(solution)/shard_map/ppermute | solution.py:151
  110.3 1.8 %collective-permute-start.4 = (bf16[4,24,2560]{2,1,0:T(8,128)(2,1)}, bf16[4,24,2560]{2,1,0:T(8,128)(2,1)S(1)}, u32[]{:S(2)}, u32[]{:S(2)}) collective-permute-start(bf16[4,24,2560]{2,1,0:T(8,128)(2,1)} %reshape.202), channel_id=1, source_target_pairs={{0,8},{4,12},{8,0},{12,4},{1,9},{5,13},{9,1},{13,5},{2,10},{6,14},... | collective-permute-start | bytes 1474568 | tf_op jit(solution)/shard_map/ppermute | solution.py:151
  112.2 5.1 %collective-permute-done.3 = bf16[4,24,2560]{2,1,0:T(8,128)(2,1)S(1)} collective-permute-done((bf16[4,24,2560]{2,1,0:T(8,128)(2,1)}, bf16[4,24,2560]{2,1,0:T(8,128)(2,1)S(1)}, u32[]{:S(2)}, u32[]{:S(2)}) %collective-permute-start.3) | collective-permute-done | bytes 491552 | tf_op jit(solution)/shard_map/ppermute | solution.py:151
  117.3 16.0 %collective-permute-done.4 = bf16[4,24,2560]{2,1,0:T(8,128)(2,1)S(1)} collective-permute-done((bf16[4,24,2560]{2,1,0:T(8,128)(2,1)}, bf16[4,24,2560]{2,1,0:T(8,128)(2,1)S(1)}, u32[]{:S(2)}, u32[]{:S(2)}) %collective-permute-start.4) | collective-permute-done | bytes 491552 | tf_op jit(solution)/shard_map/ppermute | solution.py:151
  134.0 1.6 %slice-done = s8[4194304]{0:T(1024)(128)(4,1)S(1)} async-done(((s8[7864320]{0:T(1024)(128)(4,1)}), s8[4194304]{0:T(1024)(128)(4,1)S(1)}, s32[]{:S(2)}) %slice-start) | async-done | bytes 4194328
  135.5 1.2 slice-done.1
  136.7 2.2 %fusion.46 = f32[4,96,384]{2,1,0:T(8,128)} fusion(bf16[4,96,2560]{2,1,0:T(8,128)(2,1)S(1)} %bitcast.90, bf16[4,2560,384]{2,1,0:T(8,128)(2,1)S(1)} %bitcast.92), kind=kOutput, calls=%fused_computation.140 | convolution fusion | flops 754974720 | bytes 10420224 | tf_op jit(solution)/shard_map/srj,sjd->srd/dot_general | solution.py:191
  (94 shorter events, 12.2 us)
Async XLA Ops:
  0.6 25.4 %collective-permute-start.2 = (s32[40,11]{0,1:T(8,128)}, s32[40,11]{0,1:T(8,128)S(1)}, u32[]{:S(2)}, u32[]{:S(2)}) collective-permute-start(s32[40,11]{0,1:T(8,128)} %param.14), channel_id=1, source_target_pairs={{0,4},{4,8},{8,12},{12,0},{1,5},{5,9},{9,13},{13,1},{2,6},{6,10},{... | collective-permute-start | bytes 5288 | tf_op jit(solution)/shard_map/ppermute | solution.py:151
  2.2 23.8 %collective-permute-start.1 = (s32[40,11]{0,1:T(8,128)}, s32[40,11]{0,1:T(8,128)S(1)}, u32[]{:S(2)}, u32[]{:S(2)}) collective-permute-start(s32[40,11]{0,1:T(8,128)} %param.14), channel_id=1, source_target_pairs={{0,8},{4,12},{8,0},{12,4},{1,9},{5,13},{9,1},{13,5},{2,10},{6,14},... | collective-permute-start | bytes 5288 | tf_op jit(solution)/shard_map/ppermute | solution.py:151
  4.9 21.1 %collective-permute-start = (s32[40,11]{0,1:T(8,128)}, s32[40,11]{0,1:T(8,128)S(1)}, u32[]{:S(2)}, u32[]{:S(2)}) collective-permute-start(s32[40,11]{0,1:T(8,128)} %param.14), channel_id=1, source_target_pairs={{0,12},{4,0},{8,4},{12,8},{1,13},{5,1},{9,5},{13,9},{2,14},{6,2},{... | collective-permute-start | bytes 5288 | tf_op jit(solution)/shard_map/ppermute | solution.py:151
  7.4 78.5 %collective-permute-start.6 = (f32[2,1,2176]{2,1,0:T(1,128)S(1)}, f32[2,1,2176]{2,1,0:T(1,128)S(1)}, u32[]{:S(2)}, u32[]{:S(2)}) collective-permute-start(f32[2,1,2176]{2,1,0:T(1,128)S(1)} %get-tuple-element.18), channel_id=1, source_target_pairs={{1,0},{2,1},{3,2},{16,3},{17,16},{18,17},{19,18},{32,19},{33,32},{... | collective-permute-start | bytes 52232 | tf_op jit(solution)/shard_map/ppermute | solution.py:204
  16.2 69.7 %collective-permute-start.7 = (f32[2,1,2176]{2,1,0:T(1,128)S(1)}, f32[2,1,2176]{2,1,0:T(1,128)S(1)}, u32[]{:S(2)}, u32[]{:S(2)}) collective-permute-start(f32[2,1,2176]{2,1,0:T(1,128)S(1)} %get-tuple-element.19), channel_id=1, source_target_pairs={{0,1},{1,2},{2,3},{3,16},{16,17},{17,18},{18,19},{19,32},{32,33},{... | collective-permute-start | bytes 52232 | tf_op jit(solution)/shard_map/ppermute | solution.py:203
  27.6 20.6 %copy-start = (f32[16,2176]{1,0:T(8,128)S(1)}, f32[16,2176]{1,0:T(8,128)}, u32[]{:S(2)}) copy-start(f32[16,2176]{1,0:T(8,128)} %param.15) | copy-start | bytes 417796
  27.6 20.6 %copy-start.1 = (f32[16,2176]{1,0:T(8,128)S(1)}, f32[16,2176]{1,0:T(8,128)}, u32[]{:S(2)}) copy-start(f32[16,2176]{1,0:T(8,128)} %param.16) | copy-start | bytes 417796
  41.1 16.0 %collective-permute-start.8 = (f32[4,136,128]{2,1,0:T(8,128)S(1)}, f32[4,136,128]{2,1,0:T(8,128)S(1)}, u32[]{:S(2)}, u32[]{:S(2)}) collective-permute-start(f32[4,136,128]{2,1,0:T(8,128)S(1)} %get-tuple-element.10), channel_id=1, source_target_pairs={{0,1},{1,2},{2,3},{3,16},{16,17},{17,18},{18,19},{19,32},{32,33},{... | collective-permute-start | bytes 835592 | tf_op jit(solution)/shard_map/ppermute | solution.py:195
  41.7 15.4 %collective-permute-start.9 = (f32[4,136,128]{2,1,0:T(8,128)S(1)}, f32[4,136,128]{2,1,0:T(8,128)S(1)}, u32[]{:S(2)}, u32[]{:S(2)}) collective-permute-start(f32[4,136,128]{2,1,0:T(8,128)S(1)} %get-tuple-element.11), channel_id=1, source_target_pairs={{1,0},{2,1},{3,2},{16,3},{17,16},{18,17},{19,18},{32,19},{33,32},{... | collective-permute-start | bytes 835592 | tf_op jit(solution)/shard_map/ppermute | solution.py:195
  57.9 10.2 %all-to-all-start.1 = ((f32[4,136,128]{2,1,0:T(8,128)}), f32[4,136,128]{2,1,0:T(8,128)S(1)}, u32[]{:S(2)}, u32[]{:S(2)}) async-start(f32[4,136,128]{2,1,0:T(8,128)} %fusion.9), calls=%async_computation.1 | async-start | bytes 557056 | tf_op jit(solution)/shard_map/all_to_all | solution.py:196
  68.1 12.7 %collective-permute-start.10 = (f32[136,128]{1,0:T(8,128)S(1)}, f32[136,128]{1,0:T(8,128)S(1)}, u32[]{:S(2)}, u32[]{:S(2)}) collective-permute-start(f32[136,128]{1,0:T(8,128)S(1)} %reduce_sum.9), channel_id=1, source_target_pairs={{0,12},{4,0},{8,4},{12,8},{1,13},{5,1},{9,5},{13,9},{2,14},{6,2},{... | collective-permute-start | bytes 208904 | tf_op jit(solution)/shard_map/ppermute | solution.py:151
  69.4 28.2 %all-to-all-start = ((bf16[64,8,512]{2,1,0:T(8,128)(2,1)}), bf16[64,8,512]{2,1,0:T(8,128)(2,1)S(1)}, u32[]{:S(2)}, u32[]{:S(2)}) async-start(bf16[64,8,512]{2,1,0:T(8,128)(2,1)} %get-tuple-element.6), calls=%async_computation | async-start | bytes 1048576 | tf_op jit(solution)/shard_map/all_to_all | solution.py:186
  78.7 7.1 %collective-permute-start.12 = (f32[136,128]{1,0:T(8,128)S(1)}, f32[136,128]{1,0:T(8,128)S(1)}, u32[]{:S(2)}, u32[]{:S(2)}) collective-permute-start(f32[136,128]{1,0:T(8,128)S(1)} %reduce_sum.9), channel_id=1, source_target_pairs={{0,4},{4,8},{8,12},{12,0},{1,5},{5,9},{9,13},{13,1},{2,6},{6,10},{... | collective-permute-start | bytes 208904 | tf_op jit(solution)/shard_map/ppermute | solution.py:151
  79.7 5.9 %collective-permute-start.11 = (f32[136,128]{1,0:T(8,128)S(1)}, f32[136,128]{1,0:T(8,128)S(1)}, u32[]{:S(2)}, u32[]{:S(2)}) collective-permute-start(f32[136,128]{1,0:T(8,128)S(1)} %reduce_sum.9), channel_id=1, source_target_pairs={{0,8},{4,12},{8,0},{12,4},{1,9},{5,13},{9,1},{13,5},{2,10},{6,14},... | collective-permute-start | bytes 208904 | tf_op jit(solution)/shard_map/ppermute | solution.py:151
  86.8 17.6 %copy-start.2 = (f32[16,2176]{1,0:T(8,128)}, f32[16,2176]{1,0:T(8,128)S(1)}, u32[]{:S(2)}) copy-start(f32[16,2176]{1,0:T(8,128)S(1)} %get-tuple-element.13) | copy-start | bytes 417796
  86.8 16.3 %collective-permute-start.14 = (f32[16,2176]{1,0:T(8,128)S(1)}, f32[16,2176]{1,0:T(8,128)S(1)}, u32[]{:S(2)}, u32[]{:S(2)}) collective-permute-start(f32[16,2176]{1,0:T(8,128)S(1)} %get-tuple-element.13), channel_id=1, source_target_pairs={{1,0},{2,1},{3,2},{16,3},{17,16},{18,17},{19,18},{32,19},{33,32},{... | collective-permute-start | bytes 417800 | tf_op jit(solution)/shard_map/ppermute | solution.py:212
  90.8 12.4 %collective-permute-start.13 = (f32[16,2176]{1,0:T(8,128)S(1)}, f32[16,2176]{1,0:T(8,128)S(1)}, u32[]{:S(2)}, u32[]{:S(2)}) collective-permute-start(f32[16,2176]{1,0:T(8,128)S(1)} %get-tuple-element.13), channel_id=1, source_target_pairs={{0,1},{1,2},{2,3},{3,16},{16,17},{17,18},{18,19},{19,32},{32,33},{... | collective-permute-start | bytes 417800 | tf_op jit(solution)/shard_map/ppermute | solution.py:212
  98.3 6.3 %copy-start.3 = (s32[40]{0:T(128)S(1)}, s32[40]{0:T(128)}, u32[]{:S(2)}) copy-start(s32[40]{0:T(128)} %param.10) | copy-start | bytes 484
  103.0 14.3 %collective-permute-start.3 = (bf16[4,24,2560]{2,1,0:T(8,128)(2,1)}, bf16[4,24,2560]{2,1,0:T(8,128)(2,1)S(1)}, u32[]{:S(2)}, u32[]{:S(2)}) collective-permute-start(bf16[4,24,2560]{2,1,0:T(8,128)(2,1)} %reshape.202), channel_id=1, source_target_pairs={{0,12},{4,0},{8,4},{12,8},{1,13},{5,1},{9,5},{13,9},{2,14},{6,2},{... | collective-permute-start | bytes 1474568 | tf_op jit(solution)/shard_map/ppermute | solution.py:151
  108.4 25.0 %collective-permute-start.5 = (bf16[4,24,2560]{2,1,0:T(8,128)(2,1)}, bf16[4,24,2560]{2,1,0:T(8,128)(2,1)S(1)}, u32[]{:S(2)}, u32[]{:S(2)}) collective-permute-start(bf16[4,24,2560]{2,1,0:T(8,128)(2,1)} %reshape.202), channel_id=1, source_target_pairs={{0,4},{4,8},{8,12},{12,0},{1,5},{5,9},{9,13},{13,1},{2,6},{6,10},{... | collective-permute-start | bytes 1474568 | tf_op jit(solution)/shard_map/ppermute | solution.py:151
  110.3 23.0 %collective-permute-start.4 = (bf16[4,24,2560]{2,1,0:T(8,128)(2,1)}, bf16[4,24,2560]{2,1,0:T(8,128)(2,1)S(1)}, u32[]{:S(2)}, u32[]{:S(2)}) collective-permute-start(bf16[4,24,2560]{2,1,0:T(8,128)(2,1)} %reshape.202), channel_id=1, source_target_pairs={{0,8},{4,12},{8,0},{12,4},{1,9},{5,13},{9,1},{13,5},{2,10},{6,14},... | collective-permute-start | bytes 1474568 | tf_op jit(solution)/shard_map/ppermute | solution.py:151
  133.3 2.2 %slice-start = ((s8[7864320]{0:T(1024)(128)(4,1)}), s8[4194304]{0:T(1024)(128)(4,1)S(1)}, s32[]{:S(2)}) async-start(s8[7864320]{0:T(1024)(128)(4,1)} %bitcast.91), calls=%async_computation.2 | async-start | bytes 8388608
  133.6 3.1 %slice-start.1 = ((s8[7864320]{0:T(1024)(128)(4,1)}), s8[3670016]{0:T(1024)(128)(4,1)S(1)}, s32[]{:S(2)}) async-start(s8[7864320]{0:T(1024)(128)(4,1)} %bitcast.91), calls=%async_computation.3 | async-start | bytes 7340032

commit v2 on v0

v2 whole, which is shorter than its diff:
```python
import functools
import math

import jax
import jax.numpy as jnp
import numpy as np
from jax import lax
from jax.experimental import pallas as pl
from jax.experimental.pallas import tpu as pltpu
from jax.sharding import PartitionSpec as P

BLOCK = 128
FULL_TURN = 2.0 * math.pi
DIFFUSION = 0.2
COUPLING = 0.5
CHUNK = 512
MESH = pl.DeviceIdType.MESH
F32 = jnp.float32
BF16 = jnp.bfloat16


def cos_sin(phase, length):
    quarter = length // 4
    turns = sum((phase >= quarter // 2 + i * quarter).astype(jnp.int32) for i in range(4))
    t = (phase - turns * quarter).astype(F32) * (FULL_TURN / length)
    u = t * t
    c = 1.0 + u * (-1 / 2 + u * (1 / 24 + u * (-1 / 720 + u * (1 / 40320 - u / 3628800))))
    s = t * (1.0 + u * (-1 / 6 + u * (1 / 120 + u * (-1 / 5040 + u * (1 / 362880)))))
    odd = (turns == 1) | (turns == 3)
    cos = jnp.where(odd, s, c)
    sin = jnp.where(odd, c, s)
    cos = jnp.where((turns == 1) | (turns == 2), -cos, cos)
    sin = jnp.where((turns == 2) | (turns == 3), -sin, sin)
    return cos, sin


def modulo(value, length):
    whole = jnp.floor((value.astype(F32) + 0.5) * (1.0 / length)).astype(jnp.int32)
    return value - whole * length


def local_kernel(
    lat_ref, weight_ref, x_ref, wave_ref,
    msg_ref, high_ref, low_ref,
    masked, table, acc, padded, blocks, fine, coarse, lat_col,
):
    step = pl.program_id(0)
    rows, width = x_ref.shape
    waves = wave_ref.shape[1]
    band = lat_ref.shape[0]
    pair_rows = 2 * band
    pairs = rows // pair_rows
    parts = width // BLOCK
    steps = pl.num_programs(0)
    coarse_count = coarse.shape[1]
    length = coarse_count * BLOCK
    quarter = blocks.shape[0] // 4
    quarter_blocks = coarse_count // 4

    @pl.when(step == 0)
    def _():
        wave = wave_ref[...]
        offsets = lax.broadcasted_iota(jnp.int32, (BLOCK, waves), 0)
        fine[0], fine[1] = cos_sin(modulo(offsets * wave, length), length)
        starts = lax.broadcasted_iota(jnp.int32, (coarse_count, waves), 0)
        coarse[0], coarse[1] = cos_sin(BLOCK * modulo(starts * wave, coarse_count), length)
        for j in range(band):
            row = jnp.full((1, BLOCK), lat_ref[j], jnp.int32)
            lat_col[j : j + 1, :] = row
            lat_col[band + j : band + j + 1, :] = row
        for q in range(4):
            blocks[q * quarter + quarter_blocks * band : (q + 1) * quarter, :] = jnp.zeros(
                (quarter - quarter_blocks * band, 2 * BLOCK), F32
            )

    fc, fs = fine[0], fine[1]
    for a in range(parts):
        at = step * parts + a
        cc = coarse[0, pl.ds(at, 1), :]
        cs = coarse[1, pl.ds(at, 1), :]
        table[a * BLOCK : (a + 1) * BLOCK, :waves] = (fc * cc - fs * cs).astype(BF16)
        table[a * BLOCK : (a + 1) * BLOCK, waves:] = (-(fs * cc) - fc * cs).astype(BF16)

    lanes = lax.broadcasted_iota(jnp.int32, (pair_rows, BLOCK), 1)
    upper = lax.broadcasted_iota(jnp.int32, (pair_rows, BLOCK), 0) < band
    levels = rows // (2 * band)
    for a in range(parts):
        cols = slice(a * BLOCK, (a + 1) * BLOCK)
        keep = lanes + (step * width + a * BLOCK) < lat_col[...]
        at = step * parts + a
        start = pl.multiple_of((at // quarter_blocks) * quarter + (at % quarter_blocks) * band, 8)
        for f in range(2):
            total = None
            for p in range(pairs // 2):
                here = slice((f * (pairs // 2) + p) * pair_rows, (f * (pairs // 2) + p + 1) * pair_rows)
                part = jnp.where(keep, x_ref[here, cols].astype(F32), 0.0)
                masked[here, cols] = part.astype(BF16)
                scale = jnp.where(
                    upper, weight_ref[f * levels + 2 * p], weight_ref[f * levels + 2 * p + 1]
                )
                term = part * scale
                total = term if total is None else total + term
            blocks[pl.ds(start, band), f * BLOCK : (f + 1) * BLOCK] = total[:band] + total[band:]

    product = jnp.dot(masked[...], table[...], preferred_element_type=F32)

    @pl.when(step == 0)
    def _():
        acc[...] = product

    @pl.when(step > 0)
    def _():
        acc[...] += product

    @pl.when(step == steps - 1)
    def _():
        group = 3 * band
        lat = lat_col[:band, :]
        root = 1.0 / jnp.sqrt(lat.astype(F32))
        for n in range(waves // BLOCK):
            wave = wave_ref[:, n * BLOCK : (n + 1) * BLOCK]
            weight = jnp.where(2 * wave < lat, root, 0.0)
            for c in range(2):
                cols = slice(c * waves + n * BLOCK, c * waves + (n + 1) * BLOCK)
                for fl in range(rows // band):
                    base = (fl // 3) * BLOCK + (fl % 3) * band
                    padded[base : base + band, cols] = acc[fl * band : (fl + 1) * band, cols] * weight
        for t in range(rows // group):
            padded[t * BLOCK + group : (t + 1) * BLOCK, :] = jnp.zeros((BLOCK - group, 2 * waves), F32)
        turned = padded[...].T
        total_lanes = turned.shape[1]
        real = turned[:waves].reshape(waves // 8, 8, total_lanes)
        imag = turned[waves:].reshape(waves // 8, 8, total_lanes)
        first = lax.broadcasted_iota(jnp.int32, real.shape, 1) < 4
        even = jnp.where(first, real, pltpu.roll(imag, 4, 1))
        odd = jnp.where(first, pltpu.roll(real, 4, 1), imag)
        both = jnp.stack([even, odd], axis=1).reshape(msg_ref.shape)
        msg_ref[...] = both.astype(BF16)
        high = blocks[...].astype(BF16)
        high_ref[...] = high
        low_ref[...] = (blocks[...] - high.astype(F32)).astype(BF16)


def local_part(fields, lat_points, wave_order, column_weight):
    nf, nl, band, length = fields.shape
    rows = nf * nl * band
    waves = wave_order.shape[0]
    whole = lambda shape: pl.BlockSpec(shape, lambda i, *_: (0,) * len(shape))
    lanes = rows // (3 * band) * BLOCK
    count = length // BLOCK
    outs = [((waves // 4, 8, lanes), BF16), ((2048, 2 * BLOCK), BF16), ((2048, 2 * BLOCK), BF16)]
    return pl.pallas_call(
        local_kernel,
        grid_spec=pltpu.PrefetchScalarGridSpec(
            num_scalar_prefetch=2,
            grid=(length // CHUNK,),
            in_specs=[pl.BlockSpec((rows, CHUNK), lambda i, *_: (0, i)), whole((1, waves))],
            out_specs=[whole(shape) for shape, _ in outs],
            scratch_shapes=[
                pltpu.VMEM((rows, CHUNK), BF16),
                pltpu.VMEM((CHUNK, 2 * waves), BF16),
                pltpu.VMEM((rows, 2 * waves), F32),
                pltpu.VMEM((lanes, 2 * waves), F32),
                pltpu.VMEM((2048, 2 * BLOCK), F32),
                pltpu.VMEM((2, BLOCK, waves), F32),
                pltpu.VMEM((2, count, waves), F32),
                pltpu.VMEM((2 * band, BLOCK), jnp.int32),
            ],
        ),
        out_shape=[jax.ShapeDtypeStruct(*o) for o in outs],
        compiler_params=pltpu.CompilerParams(vmem_limit_bytes=32 * 1024 * 1024),
    )(
        lat_points,
        column_weight.astype(F32).reshape(-1),
        fields.reshape(rows, length),
        wave_order.reshape(1, waves),
    )


def link_kernel(
    sizes,
    lat_ref, msg_ref, high_ref, low_ref, slot_ref, temp_ref, salt_ref, sea_ref, want_ref, leg_hbm,
    spectra_ref, temp_out, salt_out, surface_ref,
    leg, arrived, gathered, regroup, parts, sums, slots, edge_from, edge_to, fresh, fresh_half, near, near_half,
    leg_sem, a2a_send, a2a_recv, slot_send, slot_recv, edge_send, edge_recv, part_send, part_recv,
    ring_send, left_recv, right_recv, far_recv, out_send, out_recv, half_send, half_recv, own_sem,
):
    nlat, nlev, nocn = sizes
    groups = nlat * nocn
    lat_at, q, ocn_at = lax.axis_index("lat"), lax.axis_index("lev"), lax.axis_index("ocn")
    g = lat_at * nocn + ocn_at
    section = groups // 4
    high_at, low_at = g // section, g % section
    band = lat_ref.shape[0]

    def device(group, lev):
        return (group // nocn, lev, group % nocn)

    def beside(offset):
        return (g + groups + offset) % groups

    def other(k):
        return (q + k) % nlev

    leg_copy = pltpu.make_async_copy(leg_hbm, leg, leg_sem)
    leg_copy.start()

    barrier = pltpu.get_barrier_semaphore()

    def greet(k, _):
        pl.semaphore_signal(barrier, inc=1, device_id=device((g + k) % groups, q), device_id_type=MESH)
        return 0

    lax.fori_loop(1, groups, greet, 0)
    for k in range(1, nlev):
        for offset in (-1, 0, 1):
            pl.semaphore_signal(barrier, inc=1, device_id=device(beside(offset), other(k)), device_id_type=MESH)
    pl.semaphore_wait(barrier, groups - 1 + 3 * (nlev - 1))

    for k in range(1, nlev):
        pltpu.make_async_remote_copy(
            src_ref=slot_ref, dst_ref=slots.at[q], send_sem=slot_send, recv_sem=slot_recv,
            device_id=device(g, other(k)), device_id_type=MESH,
        ).start()
    pltpu.make_async_copy(slot_ref, slots.at[q], slot_recv).start()

    for h in range(4):
        def send(i, _, h=h):
            target = ((high_at + h) % 4) * section + (low_at + i) % section
            pltpu.make_async_remote_copy(
                src_ref=msg_ref.at[target], dst_ref=arrived.at[g], send_sem=a2a_send, recv_sem=a2a_recv.at[h],
                device_id=device(target, q), device_id_type=MESH,
            ).start()
            return 0

        lax.fori_loop(1 if h == 0 else 0, section, send, 0)
    pltpu.make_async_copy(msg_ref.at[g], arrived.at[g], a2a_recv.at[0]).start()

    is_temp = q < 2
    half = q % 2
    edge_row = jnp.where(half == 0, jnp.where(is_temp, temp_ref[15:16, :], salt_ref[15:16, :]),
                         jnp.where(is_temp, temp_ref[0:1, :], salt_ref[0:1, :]))
    edge_from[...] = edge_row
    edge = pltpu.make_async_remote_copy(
        src_ref=edge_from, dst_ref=edge_to, send_sem=edge_send, recv_sem=edge_recv,
        device_id=device(beside(1 - 2 * half), q), device_id_type=MESH,
    )
    edge.start()

    pltpu.make_async_copy(slots, slots, slot_recv).wait()
    part_rows = parts.shape[2]
    ids = lax.broadcasted_iota(jnp.int32, (part_rows, slots.shape[2]), 0)
    for sec in range(3):
        for h in range(2):
            base = (sec * 2 + h) * part_rows
            total = None
            for k in range(nlev):
                hot = jnp.where(slots[k] == ids + base, 1.0, 0.0).astype(BF16)
                rows = slice(k * slots.shape[2], (k + 1) * slots.shape[2])
                term = jnp.dot(hot, high_ref[rows, :], preferred_element_type=F32)
                term += jnp.dot(hot, low_ref[rows, :], preferred_element_type=F32)
                total = term if total is None else total + term
            for f in range(2):
                parts[sec, f * 2 + h] = total[:, f * BLOCK : (f + 1) * BLOCK].astype(BF16)
    for sec in range(3):
        for k in range(nlev):
            if sec == 1 and k == 0:
                continue
            pltpu.make_async_remote_copy(
                src_ref=parts.at[sec, other(k)], dst_ref=sums.at[sec, q], send_sem=part_send, recv_sem=part_recv,
                device_id=device(beside(sec - 1), other(k)), device_id_type=MESH,
            ).start()
    pltpu.make_async_copy(parts.at[1, q], sums.at[1, q], part_recv).start()

    lanes = lax.broadcasted_iota(jnp.int32, (8, BLOCK), 1)

    def regroup_chunk(h):
        source = (high_at + 4 - h) % 4
        here = arrived.at[pl.ds(source * section, section)]
        pltpu.make_async_copy(here, here, a2a_recv.at[h]).wait()

        def tile(t, _):
            for i in range(3):
                out = [None] * (section * band // BLOCK)
                for b in range(section):
                    piece = arrived[source * section + b, :, pl.ds(pl.multiple_of(t * BLOCK, BLOCK), BLOCK)].astype(F32)
                    shift = (band * (b - i)) % BLOCK
                    if shift:
                        piece = pltpu.roll(piece, shift, 1)
                    at, begin = divmod(band * b, BLOCK)
                    if begin == 0:
                        out[at] = piece
                    else:
                        out[at] = jnp.where(lanes >= begin, piece, out[at])
                        if begin + band > BLOCK:
                            out[at + 1] = piece
                row = pl.multiple_of(t * 24 + i * 8, 8)
                for n, value in enumerate(out):
                    regroup[pl.ds(row, 8), n * BLOCK : (n + 1) * BLOCK] = value
            return 0

        lax.fori_loop(0, 4, tile, 0)
        gathered[q, h] = regroup[...].astype(BF16)
        for k, sem in ((1, left_recv), (3, right_recv)):
            pltpu.make_async_remote_copy(
                src_ref=gathered.at[q, h], dst_ref=gathered.at[q, h], send_sem=ring_send, recv_sem=sem.at[h],
                device_id=device(g, other(k)), device_id_type=MESH,
            ).start()

    split = gathered.shape[2] // 2

    def forward(h):
        for origin, target, sem, rows, far in (
            (3, 1, left_recv, slice(0, split), 0),
            (1, 3, right_recv, slice(split, 2 * split), 1),
        ):
            whole = gathered.at[other(origin), h]
            pltpu.make_async_copy(whole, whole, sem.at[h]).wait()
            some = gathered.at[other(origin), h, pl.ds(far * split, split)]
            pltpu.make_async_remote_copy(
                src_ref=some, dst_ref=some, send_sem=ring_send, recv_sem=far_recv.at[far, h],
                device_id=device(g, other(target)), device_id_type=MESH,
            ).start()

    regroup_chunk(0)
    regroup_chunk(1)

    pltpu.make_async_copy(sums, sums, part_recv).wait()
    forcing = None
    for sec in range(3):
        for k in range(nlev):
            term = sums[sec, k].astype(F32)
            forcing = term if forcing is None else forcing + term
    edge.wait()
    top = pl.multiple_of(half * 8, 8)
    value = jnp.where(is_temp, temp_ref[pl.ds(top, 8), :], salt_ref[pl.ds(top, 8), :])
    inner = jnp.where(half == 0, jnp.where(is_temp, temp_ref[8:9, :], salt_ref[8:9, :]),
                      jnp.where(is_temp, temp_ref[7:8, :], salt_ref[7:8, :]))
    outside = ((half == 0) & (g == 0)) | ((half == 1) & (g == groups - 1))
    outer = jnp.where(outside, 0.0, edge_to[...])
    above = jnp.where(half == 0, outer, inner)
    below = jnp.where(half == 0, inner, outer)
    cols = value.shape[1]
    rows8 = lax.broadcasted_iota(jnp.int32, value.shape, 0)
    north = jnp.where(rows8 == 0, jnp.broadcast_to(above, value.shape), pltpu.roll(value, 1, 0))
    south = jnp.where(rows8 == 7, jnp.broadcast_to(below, value.shape), pltpu.roll(value, 7, 0))
    laplace = south + north + pltpu.roll(value, 1, 1) + pltpu.roll(value, cols - 1, 1) - 4.0 * value
    moved = value + DIFFUSION * laplace
    sea = sea_ref[pl.ds(top, 8), :].astype(F32) * COUPLING
    for c in range(cols // BLOCK):
        new = moved[:, c * BLOCK : (c + 1) * BLOCK] + jnp.broadcast_to(sea[:, c : c + 1], (8, BLOCK)) * forcing[c * 8 : (c + 1) * 8]
        fresh[c * 8 : (c + 1) * 8, :] = new
    fresh_half[...] = fresh[...].astype(BF16)
    for k in range(1, nlev):
        pltpu.make_async_remote_copy(
            src_ref=fresh, dst_ref=near.at[q], send_sem=out_send, recv_sem=out_recv,
            device_id=device(g, other(k)), device_id_type=MESH,
        ).start()
    pltpu.make_async_copy(fresh, near.at[q], out_recv).start()

    @pl.when(is_temp)
    def _():
        for k in range(nlev):
            for side in range(2):
                pltpu.make_async_remote_copy(
                    src_ref=fresh_half, dst_ref=near_half.at[side, q], send_sem=half_send, recv_sem=half_recv,
                    device_id=device(beside(1 - 2 * side), other(k)), device_id_type=MESH,
                ).start()

    forward(0)
    regroup_chunk(2)
    forward(1)
    regroup_chunk(3)

    columns = want_ref.shape[0]
    perm = jnp.where(
        want_ref[...] == lax.broadcasted_iota(jnp.int32, (columns, columns), 1), 1.0, 0.0
    ).astype(BF16)

    def contract(h):
        for far, origin in ((0, 2), (1, 2)):
            some = gathered.at[other(origin), h, pl.ds(far * split, split)]
            pltpu.make_async_copy(some, some, far_recv.at[far, h]).wait()
        whole = jnp.concatenate([gathered[k, h] for k in range(nlev)], axis=0)
        ordered = jnp.dot(perm, whole, preferred_element_type=F32).astype(BF16)
        source = (high_at + 4 - h) % 4
        depth = section * band
        each = columns // 4
        for s in range(4):
            term = jnp.dot(
                ordered[s * each : (s + 1) * each],
                leg[s, pl.ds(pl.multiple_of(source * depth, 128), depth), :],
                preferred_element_type=F32,
            )
            spectra_ref[s] = term if h == 0 else spectra_ref[s] + term

    forward(2)
    leg_copy.wait()
    contract(0)
    forward(3)
    contract(1)

    pltpu.make_async_copy(near, near, out_recv).wait()
    pltpu.make_async_copy(near_half, near_half, half_recv).wait()
    for h in range(2):
        for c in range(cols // BLOCK):
            temp_out[h * 8 : (h + 1) * 8, c * BLOCK : (c + 1) * BLOCK] = near[h, c * 8 : (c + 1) * 8, :]
            salt_out[h * 8 : (h + 1) * 8, c * BLOCK : (c + 1) * BLOCK] = near[2 + h, c * 8 : (c + 1) * 8, :]
    mine = jnp.broadcast_to(slot_ref[...].astype(F32), (BLOCK, slot_ref.shape[1])).T
    blocks = surface_ref.shape[1] // BLOCK
    mine = mine[: blocks * band, :1]
    tiles = lax.broadcasted_iota(jnp.int32, (blocks * band, part_rows), 1).astype(F32)
    surface = None
    for sec in range(3):
        for h in range(2):
            hot = jnp.where(mine == tiles + float((sec * 2 + h) * part_rows), 1.0, 0.0).astype(BF16)
            if sec == 1:
                cells = near[h].astype(BF16)
            else:
                cells = near_half[sec // 2, h]
            term = jnp.dot(hot, cells, preferred_element_type=F32)
            surface = term if surface is None else surface + term
    row_lanes = lax.broadcasted_iota(jnp.int32, (1, BLOCK), 1)
    first_point = q * (blocks * BLOCK)
    for b in range(blocks):
        points = row_lanes + (first_point + b * BLOCK)
        keep = points < lat_ref[...]
        surface_ref[:, b * BLOCK : (b + 1) * BLOCK] = jnp.where(keep, surface[b * band : (b + 1) * band], 0.0)

    contract(2)
    contract(3)

    for k in range(1, nlev):
        pltpu.make_async_copy(slot_ref, slots.at[k], slot_send).wait()
    some = msg_ref.at[pl.ds(0, groups - 1)]
    pltpu.make_async_copy(some, some, a2a_send).wait()
    for k in range(3 * nlev - 1):
        pltpu.make_async_copy(parts.at[0, 0], sums.at[0, 0], part_send).wait()
    three = gathered.at[pl.ds(0, 3)]
    pltpu.make_async_copy(three, three, ring_send).wait()
    for k in range(1, nlev):
        pltpu.make_async_copy(fresh, near.at[0], out_send).wait()

    @pl.when(is_temp)
    def _():
        for k in range(2 * nlev):
            pltpu.make_async_copy(fresh_half, near_half.at[0, 0], half_send).wait()


def body(
    sizes,
    atmos_fields,
    lat_points,
    wave_order,
    legendre,
    column_weight,
    block_remap,
    ocean_temp,
    ocean_salt,
    sea_mask,
):
    nlat, nlev, nocn = sizes
    nf, nl, band, length = atmos_fields.shape
    g = lax.axis_index("lat") * nocn + lax.axis_index("ocn")
    orow, ocols = ocean_temp.shape
    tcols = ocols // BLOCK
    tile_count = orow * tcols
    part_rows = tile_count // 2
    local = block_remap - (g - 1) * tile_count
    sec, inside = local // tile_count, local % tile_count
    r, c = inside // tcols, inside % tcols
    slot = sec * tile_count + (r // 8) * part_rows + c * 8 + r % 8
    slot = slot.T.reshape(1, -1)
    slot = jnp.pad(slot, ((0, 0), (0, 512 - slot.shape[1])), constant_values=-1)
    msg, high, low = local_part(atmos_fields, lat_points, wave_order, column_weight)

    s, lev, f, c = np.meshgrid(np.arange(4), np.arange(nlev * nl), np.arange(nf), np.arange(2), indexing="ij")
    want = ((lev // nl) * nf * nl + f * nl + lev % nl) * 8 + c * 4 + s
    want = jnp.asarray(want.reshape(-1, 1), jnp.int32)

    each, nj, degrees = legendre.shape
    vm = pl.BlockSpec(memory_space=pltpu.VMEM)
    depth = nj // 4
    sem = pltpu.SemaphoreType.DMA
    quarter = length // nlev
    return pl.pallas_call(
        functools.partial(link_kernel, sizes),
        in_specs=[vm] * 9 + [pl.BlockSpec(memory_space=pl.ANY)],
        out_specs=[vm] * 4,
        out_shape=[
            jax.ShapeDtypeStruct((each, nlev * nl * nf * 2, degrees), F32),
            jax.ShapeDtypeStruct((orow, ocols), F32),
            jax.ShapeDtypeStruct((orow, ocols), F32),
            jax.ShapeDtypeStruct((band, quarter), F32),
        ],
        scratch_shapes=[
            pltpu.VMEM(legendre.shape, BF16),
            pltpu.VMEM(msg.shape, BF16),
            pltpu.VMEM((nlev, 4, nl * nf * 8, depth), BF16),
            pltpu.VMEM((nl * nf * 8, depth), F32),
            pltpu.VMEM((3, nlev, part_rows, BLOCK), BF16),
            pltpu.VMEM((3, nlev, part_rows, BLOCK), BF16),
            pltpu.VMEM((nlev, 1, 512), jnp.int32),
            pltpu.VMEM((1, ocols), F32),
            pltpu.VMEM((1, ocols), F32),
            pltpu.VMEM((part_rows, BLOCK), F32),
            pltpu.VMEM((part_rows, BLOCK), BF16),
            pltpu.VMEM((nlev, part_rows, BLOCK), F32),
            pltpu.VMEM((2, 2, part_rows, BLOCK), BF16),
            sem, sem, sem((4,)), sem, sem, sem, sem, sem, sem,
            sem, sem((4,)), sem((4,)), sem((2, 4)), sem, sem, sem, sem, sem,
        ],
        compiler_params=pltpu.CompilerParams(
            collective_id=0, has_side_effects=True, vmem_limit_bytes=40 * 1024 * 1024
        ),
    )(
        lat_points.reshape(band, 1), msg, high, low, slot, ocean_temp, ocean_salt, sea_mask, want, legendre,
    )


def solution(mesh):
    both = ("lat", "ocn")
    placed = (
        P(None, "lev", both, None),
        P(both),
        P(),
        P(both, None, "lev"),
        P(None, "lev"),
        P(both, "lev"),
        P(both, None),
        P(both, None),
        P(both, None),
    )
    sizes = tuple(mesh.shape[a] for a in ("lat", "lev", "ocn"))
    return jax.shard_map(
        functools.partial(body, sizes),
        mesh=mesh,
        in_specs=placed,
        out_specs=(P(both, None, "lev"), P(both, None), P(both, None), P(both, "lev")),
        check_vma=False,
    )
```

time: 200 us -> 78.8 us (0.39)
  waiting for transfers between devices: 74 us -> 0 us
  Pallas kernels: 0 us -> 60.9 us
  starting transfers between devices: 39.6 us -> 0 us
  other arithmetic: 37.9 us -> 0.73 us
  matrix products: 14.2 us -> 0 us
  between operations: 14.2 us -> 0.68 us
  local copies, waits for them, and re-layouts: 18.2 us -> 14.9 us
    pallas_call x0 -> x2, Pallas kernels: none -> 60.9 us  [the longest x1 51.7 us: body(): pl.pallas_call(functools.partial(link_kernel, sizes), in_specs=[vm] * 9 +...]
    psum x2 -> x0, waiting for transfers between devices: 33.4 us -> none  [the longest x1 22.7 us: body(): tile_sums = lax.psum(arrived, 'lev')]
    ppermute x6 -> x0, waiting for transfers between devices: 29.2 us -> none  [the longest x3 20.8 us: with_halo(): lax.ppermute(tail, axis, [(i, (i + 1) % count) for i in range(ends)])]
    ppermute x6 -> x0, starting transfers between devices: 27.5 us -> none  [the longest x3 21.7 us: with_halo(): lax.ppermute(head, axis, [((i + 1) % count, i) for i in range(ends)])]
    another operation x4 -> x0, other arithmetic: 25.3 us -> none
    dot_general x3 -> x0, matrix products: 14.2 us -> none  [the longest x1 6.05 us: body(): jnp.einsum('srj,sjd->srd', lax.all_gather(regrouped, 'lev', axis=1, tiled...]
    all_to_all x1 -> x0, starting transfers between devices: 12 us -> none  [body(): lax.all_to_all(coeffs.transpose(4, 1, 0, 3, 2).reshape(wave_count, lev_de...]
    all_gather x1 -> x0, waiting for transfers between devices: 11.3 us -> none  [body(): lax.all_gather(regrouped, 'lev', axis=1, tiled=True)]
  transfers between devices with their start and end apart: 10 -> 0, of which waited for: 7 -> 0; matrix products, arithmetic and copies ran while one was open for 26% -> 0% of each run, Pallas kernels for 0% -> 0%
where the time goes in v2:
time: 78.8 us; the launch traced here: 77.3 us
  Pallas kernels  60.9 us (77%)
  local copies, waits for them, and re-layouts  14.9 us (19%)
    pallas_call x1, Pallas kernels, body(): pl.pallas_call(functools.partial(link_kernel, sizes), in_specs=[vm] * 9 +...  51.7 us
    unnamed x20, local copies, waits for them, and re-layouts  13.3 us
    pallas_call x1, Pallas kernels, local_part(): pl.pallas_call(local_kernel, grid_spec=pltpu.PrefetchScalarGridSpec(num_s...  9.22 us

profile of v2, /device:TPU:32, one launch (start us, length us, event | category | flops | bytes accessed | tf_op | source)
XLA Modules:
  0.0 77.3 jit_solution(1104011558893221534)
XLA Ops:
  0.6 0.7 reshape.32.weight_ref
  1.4 0.7 fusion.4
  2.1 0.1 reshape.30
  2.2 0.7 copy.14.lat_ref
  3.0 0.0 copy-start.1
  3.0 2.5 %copy-done.1 = bf16[2,6,40,5632]{3,2,1,0:T(8,128)(2,1)S(1)} copy-done((bf16[2,6,40,5632]{3,2,1,0:T(8,128)(2,1)S(1)}, bf16[2,6,40,5632]{3,2,1,0:T(8,128)(2,1)}, u32[]{:S(2)}) %copy-start.1) | copy-done | bytes 5406744
  5.5 0.0 copy-start.6
  5.5 0.7 copy-done.6
  6.1 0.0 copy-start.7
  6.1 0.7 copy-done.7
  6.8 9.2 %shard_map.129 = (bf16[64,8,512]{2,1,0:T(8,128)(2,1)S(1)}, bf16[2048,256]{1,0:T(8,128)(2,1)S(1)}, bf16[2048,256]{1,0:T(8,128)(2,1)S(1)}) custom-call(s32[40]{0:T(128)S(1)} %copy-done.6, f32[12]{0:T(128)S(1)} %reshape.32.weight_ref, bf16[480,5632]{1,0:T(8,128)(2,1)S(1)} %bitcast.5, s32[1,256]{1,0:T(1,128)S(1)} %bitcast.7), custom_call_target="tpu_custom_call" | custom-call | tf_op jit(solution)/shard_map/pallas_call | solution.py:152
  16.0 0.0 copy-start
  16.1 3.2 %copy-done = bf16[4,2560,384]{2,1,0:T(8,128)(2,1)S(1)} copy-done((bf16[4,2560,384]{2,1,0:T(8,128)(2,1)S(1)}, bf16[4,2560,384]{2,1,0:T(8,128)(2,1)}, u32[]{:S(2)}) %copy-start) | copy-done | bytes 7864344
  19.3 0.0 copy-start.2
  19.3 0.9 %copy-done.2 = s32[384,1]{1,0:T(8,128)S(1)} copy-done((s32[384,1]{1,0:T(8,128)S(1)}, s32[384,1]{1,0:T(8,128)}, u32[]{:S(2)}) %copy-start.2) | copy-done | bytes 1560
  20.2 0.0 copy-start.3
  20.2 0.9 %copy-done.3 = f32[16,2176]{1,0:T(8,128)S(1)} copy-done((f32[16,2176]{1,0:T(8,128)S(1)}, f32[16,2176]{1,0:T(8,128)}, u32[]{:S(2)}) %copy-start.3) | copy-done | bytes 139288
  21.1 0.0 copy-start.4
  21.1 0.9 %copy-done.4 = f32[16,2176]{1,0:T(8,128)S(1)} copy-done((f32[16,2176]{1,0:T(8,128)S(1)}, f32[16,2176]{1,0:T(8,128)}, u32[]{:S(2)}) %copy-start.4) | copy-done | bytes 139288
  22.0 0.0 copy-start.5
  22.0 0.7 copy-done.5
  22.7 51.7 %shard_map.130 = (f32[4,96,384]{2,1,0:T(8,128)S(1)}, f32[16,2176]{1,0:T(8,128)S(1)}, f32[16,2176]{1,0:T(8,128)S(1)}, f32[40,1408]{1,0:T(8,128)S(1)}) custom-call(s32[40,1]{1,0:T(8,128)S(1)} %copy.14.lat_ref, bf16[64,8,512]{2,1,0:T(8,128)(2,1)S(1)} %get-tuple-element.7.msg_ref, bf16[2048,256]{1,0:T(8,128)(2,1)S(1)} %get-tuple-element.8.high_ref, ...), custom_call_target="tpu_custom_call" | custom-call | tf_op jit(solution)/shard_map/pallas_call | solution.py:486
  74.4 0.8 %copy.19 = f32[4,96,384]{2,1,0:T(8,128)} copy(f32[4,96,384]{2,1,0:T(8,128)S(1)} %get-tuple-element.14) | data formatting | bytes 1179648
  75.3 0.7 copy.20
  75.9 0.7 copy.21
  76.6 0.7 copy.22
  (1 shorter events, 0.0 us)
Async XLA Ops:
  3.0 2.5 %copy-start.1 = (bf16[2,6,40,5632]{3,2,1,0:T(8,128)(2,1)S(1)}, bf16[2,6,40,5632]{3,2,1,0:T(8,128)(2,1)}, u32[]{:S(2)}) copy-start(bf16[2,6,40,5632]{3,2,1,0:T(8,128)(2,1)} %param.10) | copy-start | bytes 16220164
  5.5 0.7 copy-start.6
  6.1 0.7 copy-start.7
  16.0 3.2 %copy-start = (bf16[4,2560,384]{2,1,0:T(8,128)(2,1)S(1)}, bf16[4,2560,384]{2,1,0:T(8,128)(2,1)}, u32[]{:S(2)}) copy-start(bf16[4,2560,384]{2,1,0:T(8,128)(2,1)} %leg_hbm.1) | copy-start | bytes 23592964
  19.3 0.9 %copy-start.2 = (s32[384,1]{1,0:T(8,128)S(1)}, s32[384,1]{1,0:T(8,128)}, u32[]{:S(2)}) copy-start(s32[384,1]{1,0:T(8,128)} %constant.72.clone.want_ref) | copy-start | bytes 4612
  20.2 0.9 %copy-start.3 = (f32[16,2176]{1,0:T(8,128)S(1)}, f32[16,2176]{1,0:T(8,128)}, u32[]{:S(2)}) copy-start(f32[16,2176]{1,0:T(8,128)} %temp_ref.1) | copy-start | bytes 417796
  21.1 0.9 %copy-start.4 = (f32[16,2176]{1,0:T(8,128)S(1)}, f32[16,2176]{1,0:T(8,128)}, u32[]{:S(2)}) copy-start(f32[16,2176]{1,0:T(8,128)} %salt_ref.1) | copy-start | bytes 417796
  22.0 0.7 copy-start.5

commit v3 on v2

v3 whole, which is shorter than its diff:
```python
import functools
import math

import jax
import jax.numpy as jnp
from jax import lax
from jax.experimental import pallas as pl
from jax.experimental.pallas import tpu as pltpu
from jax.sharding import PartitionSpec as P

BLOCK = 128
FULL_TURN = 2.0 * math.pi
DIFFUSION = 0.2
COUPLING = 0.5
CHUNK = 512
MESH = pl.DeviceIdType.MESH
F32 = jnp.float32
BF16 = jnp.bfloat16


def cos_sin(phase, length):
    quarter = length // 4
    turns = sum((phase >= quarter // 2 + i * quarter).astype(jnp.int32) for i in range(4))
    t = (phase - turns * quarter).astype(F32) * (FULL_TURN / length)
    u = t * t
    c = 1.0 + u * (-1 / 2 + u * (1 / 24 + u * (-1 / 720 + u * (1 / 40320 - u / 3628800))))
    s = t * (1.0 + u * (-1 / 6 + u * (1 / 120 + u * (-1 / 5040 + u * (1 / 362880)))))
    odd = (turns == 1) | (turns == 3)
    cos = jnp.where(odd, s, c)
    sin = jnp.where(odd, c, s)
    cos = jnp.where((turns == 1) | (turns == 2), -cos, cos)
    sin = jnp.where((turns == 2) | (turns == 3), -sin, sin)
    return cos, sin


def modulo(value, length):
    whole = jnp.floor((value.astype(F32) + 0.5) * (1.0 / length)).astype(jnp.int32)
    return value - whole * length


def fused_kernel(
    sizes,
    lat_hbm, wave_hbm, weight_hbm, remap_hbm, x_hbm, temp_hbm, salt_hbm, sea_hbm, leg_hbm,
    spectra_hbm, temp_to, salt_to, surface_to,
    spectra_ref, temp_out, salt_out, surface_ref, store_sem,
    lat_ref, wave_ref, weight_ref, remap_ref, x_ref, temp_ref, salt_ref, sea_ref, leg,
    table_a, table_b, acc, padded, blocks, block_pair, fine, coarse, lat_col, by_block_slots, slot_own, msg,
    arrived, gathered, regroup, parts, sums, slots, edge_from, edge_to, fresh, near, half_from, near_half,
    small_sem, x_sem, leg_sem, a2a_send, a2a_recv, slot_send, slot_recv, edge_send, edge_recv, part_send, part_recv,
    ring_send, left_recv, right_recv, far_recv, out_send, out_recv, half_send, half_recv,
):
    nlat, nlev, nocn = sizes
    groups = nlat * nocn
    lat_at, q, ocn_at = lax.axis_index("lat"), lax.axis_index("lev"), lax.axis_index("ocn")
    g = lat_at * nocn + ocn_at
    section = groups // 4
    high_at, low_at = g // section, g % section
    band = lat_hbm.shape[0]
    steps, rows, width = x_ref.shape
    waves = wave_ref.shape[1]
    pair_rows = 2 * band
    pairs = rows // pair_rows
    levels = rows // (2 * band)
    pieces = width // BLOCK
    length = steps * width
    count = length // BLOCK
    lane_blocks = count // nlev

    def device(group, lev):
        return (group // nocn, lev, group % nocn)

    def beside(offset):
        return (g + groups + offset) % groups

    def other(k):
        return (q + k) % nlev

    small = [
        pltpu.make_async_copy(a, b, small_sem.at[n])
        for n, (a, b) in enumerate(
            (
                (lat_hbm, lat_ref), (wave_hbm, wave_ref), (weight_hbm, weight_ref), (remap_hbm, remap_ref),
                (temp_hbm, temp_ref), (salt_hbm, salt_ref), (sea_hbm, sea_ref),
            )
        )
    ]
    for copy in small:
        copy.start()

    def x_copy(i):
        return pltpu.make_async_copy(
            x_hbm.at[:, pl.ds(pl.multiple_of(i * width, BLOCK), width)], x_ref.at[i], x_sem.at[i]
        )

    def start_x(i, _):
        x_copy(i).start()
        return 0

    lax.fori_loop(0, steps, start_x, 0)
    leg_copy = pltpu.make_async_copy(leg_hbm, leg, leg_sem)
    leg_copy.start()

    barrier = pltpu.get_barrier_semaphore()

    def greet(k, _):
        pl.semaphore_signal(barrier, inc=1, device_id=device((g + k) % groups, q), device_id_type=MESH)
        return 0

    lax.fori_loop(1, groups, greet, 0)
    for k in range(1, nlev):
        for offset in (-1, 0, 1):
            pl.semaphore_signal(barrier, inc=1, device_id=device(beside(offset), other(k)), device_id_type=MESH)

    for copy in small:
        copy.wait()
    for j in range(band):
        row = jnp.full((1, BLOCK), lat_ref[j], jnp.int32)
        lat_col[j : j + 1, :] = row
        lat_col[band + j : band + j + 1, :] = row
    wave = wave_ref[...]
    offsets = lax.broadcasted_iota(jnp.int32, (BLOCK, waves), 0)
    fine[0], fine[1] = cos_sin(modulo(offsets * wave, length), length)
    starts = lax.broadcasted_iota(jnp.int32, (count, waves), 0)
    coarse[0], coarse[1] = cos_sin(BLOCK * modulo(starts * wave, count), length)

    group = 3 * band
    tiles_row = slot_own.shape[1] // BLOCK
    per_lev = slot_own.shape[1]
    for k in range(nlev):
        for t in range(tiles_row):
            used = min(3, lane_blocks - 3 * t) * band
            start = k * per_lev + t * BLOCK + used
            blocks[start : k * per_lev + (t + 1) * BLOCK, :] = jnp.zeros((BLOCK - used, 2 * BLOCK), F32)

    orow, ocols = temp_ref.shape
    tcols = ocols // BLOCK
    tile_count = orow * tcols
    part_rows = tile_count // 2
    local = remap_ref[...] - (g - 1) * tile_count
    sec = (local >= tile_count).astype(jnp.int32) + (local >= 2 * tile_count).astype(jnp.int32)
    inside = local - sec * tile_count
    r = jnp.floor((inside.astype(F32) + 0.5) * (1.0 / tcols)).astype(jnp.int32)
    c = inside - r * tcols
    low_half = (r >= 8).astype(jnp.int32)
    slot = sec * tile_count + low_half * part_rows + c * 8 + r - 8 * low_half
    by_block_slots[...] = jnp.zeros(by_block_slots.shape, F32)
    by_block_slots[:lane_blocks, :band] = slot.astype(F32)
    by_block = by_block_slots[...]
    moved_slots = [by_block, pltpu.roll(by_block, band, 1), pltpu.roll(by_block, 2 * band, 1)]
    lane_row = lax.broadcasted_iota(jnp.int32, (1, BLOCK), 1)
    for t in range(tiles_row):
        row = jnp.full((1, BLOCK), -1.0, F32)
        for i in range(3):
            b = 3 * t + i
            if b < lane_blocks:
                here = (lane_row >= band * i) & (lane_row < band * (i + 1))
                row = jnp.where(here, moved_slots[i][b : b + 1], row)
        slot_own[:, t * BLOCK : (t + 1) * BLOCK] = row.astype(jnp.int32)

    pair_lanes = lax.broadcasted_iota(jnp.int32, (pair_rows, BLOCK), 1)
    upper = lax.broadcasted_iota(jnp.int32, (pair_rows, BLOCK), 0) < band
    weights = weight_ref[...].astype(F32)
    scales = [
        [
            jnp.where(upper, weights[f : f + 1, 2 * p : 2 * p + 1], weights[f : f + 1, 2 * p + 1 : 2 * p + 2])
            for p in range(pairs // 2)
        ]
        for f in range(2)
    ]

    def mask_step(step, _):
        x_copy(step).wait()
        for a in range(pieces):
            cols = slice(a * BLOCK, (a + 1) * BLOCK)
            keep = pair_lanes + (step * width + a * BLOCK) < lat_col[...]
            at = step * pieces + a
            inner = at % lane_blocks
            start = (at // lane_blocks) * per_lev + (inner // 3) * BLOCK + (inner % 3) * band
            start = pl.multiple_of(start, 8)
            for f in range(2):
                total = None
                for p in range(pairs // 2):
                    here = slice((f * (pairs // 2) + p) * pair_rows, (f * (pairs // 2) + p + 1) * pair_rows)
                    part = jnp.where(keep, x_ref[step, here, cols].astype(F32), 0.0)
                    x_ref[step, here, cols] = part.astype(BF16)
                    term = part * scales[f][p]
                    total = term if total is None else total + term
                blocks[pl.ds(start, band), f * BLOCK : (f + 1) * BLOCK] = total[:band] + total[band:]
        return 0

    early = 4
    lax.fori_loop(0, early, mask_step, 0)

    pl.semaphore_wait(barrier, groups - 1 + 3 * (nlev - 1))
    for k in range(1, nlev):
        pltpu.make_async_remote_copy(
            src_ref=slot_own, dst_ref=slots.at[q], send_sem=slot_send, recv_sem=slot_recv,
            device_id=device(g, other(k)), device_id_type=MESH,
        ).start()
    pltpu.make_async_copy(slot_own, slots.at[q], slot_recv).start()
    is_temp = q < 2
    half = q % 2
    edge_from[...] = jnp.where(
        half == 0,
        jnp.where(is_temp, temp_ref[orow - 1 : orow, :], salt_ref[orow - 1 : orow, :]),
        jnp.where(is_temp, temp_ref[0:1, :], salt_ref[0:1, :]),
    )
    edge = pltpu.make_async_remote_copy(
        src_ref=edge_from, dst_ref=edge_to, send_sem=edge_send, recv_sem=edge_recv,
        device_id=device(beside(1 - 2 * half), q), device_id_type=MESH,
    )
    edge.start()

    lax.fori_loop(early, steps, mask_step, 0)

    high = blocks[...].astype(BF16)
    block_pair[:, : 2 * BLOCK] = high
    block_pair[:, 2 * BLOCK :] = (blocks[...] - high.astype(F32)).astype(BF16)
    pltpu.make_async_copy(slots, slots, slot_recv).wait()
    all_slots = jnp.concatenate([slots[k] for k in range(nlev)], axis=1)
    ids = lax.broadcasted_iota(jnp.int32, (part_rows, all_slots.shape[1]), 0)
    for sec in range(3):
        for h in range(2):
            hot = jnp.where(all_slots == ids + (sec * 2 + h) * part_rows, 1.0, 0.0).astype(BF16)
            total = jnp.dot(hot, block_pair[...], preferred_element_type=F32)
            for f in range(2):
                both = total[:, f * BLOCK : (f + 1) * BLOCK] + total[:, (2 + f) * BLOCK : (3 + f) * BLOCK]
                parts[sec, f * 2 + h] = both.astype(BF16)
        for k in range(nlev):
            if sec == 1 and k == 0:
                continue
            pltpu.make_async_remote_copy(
                src_ref=parts.at[sec, other(k)], dst_ref=sums.at[sec, q], send_sem=part_send, recv_sem=part_recv,
                device_id=device(beside(sec - 1), other(k)), device_id_type=MESH,
            ).start()
    pltpu.make_async_copy(parts.at[1, q], sums.at[1, q], part_recv).start()

    def make_table(table, step):
        fc, fs = fine[0], fine[1]
        for a in range(pieces):
            cc = coarse[0, pl.ds(step * pieces + a, 1), :]
            cs = coarse[1, pl.ds(step * pieces + a, 1), :]
            table[a * BLOCK : (a + 1) * BLOCK, :waves] = (fc * cc - fs * cs).astype(BF16)
            table[a * BLOCK : (a + 1) * BLOCK, waves:] = (-(fs * cc) - fc * cs).astype(BF16)

    make_table(table_a, 0)
    acc[...] = jnp.zeros(acc.shape, F32)

    def two_steps(i, _):
        make_table(table_b, 2 * i + 1)
        acc[...] += jnp.dot(x_ref[2 * i], table_a[...], preferred_element_type=F32)
        make_table(table_a, 2 * i + 2)
        acc[...] += jnp.dot(x_ref[2 * i + 1], table_b[...], preferred_element_type=F32)
        return 0

    lax.fori_loop(0, steps // 2, two_steps, 0)
    acc[...] += jnp.dot(x_ref[steps - 1], table_a[...], preferred_element_type=F32)

    lat = lat_col[:band, :]
    root = 1.0 / jnp.sqrt(lat.astype(F32))
    for n in range(waves // BLOCK):
        weight = jnp.where(2 * wave_ref[:, n * BLOCK : (n + 1) * BLOCK] < lat, root, 0.0)
        for c in range(2):
            cols = slice(c * waves + n * BLOCK, c * waves + (n + 1) * BLOCK)
            for fl in range(rows // band):
                base = (fl // 3) * BLOCK + (fl % 3) * band
                padded[base : base + band, cols] = acc[fl * band : (fl + 1) * band, cols] * weight
    for t in range(rows // group):
        padded[t * BLOCK + group : (t + 1) * BLOCK, :] = jnp.zeros((BLOCK - group, 2 * waves), F32)
    turned = padded[...].T
    real = turned[:waves].reshape(waves // 8, 8, turned.shape[1])
    imag = turned[waves:].reshape(waves // 8, 8, turned.shape[1])
    first = lax.broadcasted_iota(jnp.int32, real.shape, 1) < 4
    even = jnp.where(first, real, pltpu.roll(imag, 4, 1))
    odd = jnp.where(first, pltpu.roll(real, 4, 1), imag)
    msg[...] = jnp.stack([even, odd], axis=1).reshape(msg.shape).astype(BF16)

    for h in range(4):
        def send(i, _, h=h):
            target = ((high_at + h) % 4) * section + (low_at + i) % section
            pltpu.make_async_remote_copy(
                src_ref=msg.at[target], dst_ref=arrived.at[g], send_sem=a2a_send, recv_sem=a2a_recv.at[h],
                device_id=device(target, q), device_id_type=MESH,
            ).start()
            return 0

        lax.fori_loop(1 if h == 0 else 0, section, send, 0)
    pltpu.make_async_copy(msg.at[g], arrived.at[g], a2a_recv.at[0]).start()

    pltpu.make_async_copy(sums, sums, part_recv).wait()
    forcing = None
    for sec in range(3):
        for k in range(nlev):
            term = sums[sec, k].astype(F32)
            forcing = term if forcing is None else forcing + term
    edge.wait()
    top = pl.multiple_of(half * 8, 8)
    value = jnp.where(is_temp, temp_ref[pl.ds(top, 8), :], salt_ref[pl.ds(top, 8), :])
    inner = jnp.where(
        half == 0,
        jnp.where(is_temp, temp_ref[8:9, :], salt_ref[8:9, :]),
        jnp.where(is_temp, temp_ref[7:8, :], salt_ref[7:8, :]),
    )
    outside = ((half == 0) & (g == 0)) | ((half == 1) & (g == groups - 1))
    outer = jnp.where(outside, 0.0, edge_to[...])
    above = jnp.where(half == 0, outer, inner)
    below = jnp.where(half == 0, inner, outer)
    rows8 = lax.broadcasted_iota(jnp.int32, value.shape, 0)
    north = jnp.where(rows8 == 0, jnp.broadcast_to(above, value.shape), pltpu.roll(value, 1, 0))
    south = jnp.where(rows8 == 7, jnp.broadcast_to(below, value.shape), pltpu.roll(value, 7, 0))
    laplace = south + north + pltpu.roll(value, 1, 1) + pltpu.roll(value, ocols - 1, 1) - 4.0 * value
    moved = value + DIFFUSION * laplace
    sea = sea_ref[pl.ds(top, 8), :].astype(F32) * COUPLING
    for c in range(tcols):
        here = slice(c * 8, (c + 1) * 8)
        fresh[here, :] = (
            moved[:, c * BLOCK : (c + 1) * BLOCK] + jnp.broadcast_to(sea[:, c : c + 1], (8, BLOCK)) * forcing[here]
        )
    for k in range(1, nlev):
        pltpu.make_async_remote_copy(
            src_ref=fresh, dst_ref=near.at[q], send_sem=out_send, recv_sem=out_recv,
            device_id=device(g, other(k)), device_id_type=MESH,
        ).start()
    pltpu.make_async_copy(fresh, near.at[q], out_recv).start()

    lanes = lax.broadcasted_iota(jnp.int32, (8, BLOCK), 1)

    def regroup_chunk(h):
        source = (high_at + 4 - h) % 4
        here = arrived.at[pl.ds(source * section, section)]
        pltpu.make_async_copy(here, here, a2a_recv.at[h]).wait()

        def tile(t, _):
            for i in range(3):
                out = [None] * (section * band // BLOCK)
                for b in range(section):
                    piece = arrived[source * section + b, :, pl.ds(pl.multiple_of(t * BLOCK, BLOCK), BLOCK)].astype(F32)
                    shift = (band * (b - i)) % BLOCK
                    if shift:
                        piece = pltpu.roll(piece, shift, 1)
                    at, begin = divmod(band * b, BLOCK)
                    if begin == 0:
                        out[at] = piece
                    else:
                        out[at] = jnp.where(lanes >= begin, piece, out[at])
                        if begin + band > BLOCK:
                            out[at + 1] = piece
                row = pl.multiple_of(t * 24 + i * 8, 8)
                for n, tile_value in enumerate(out):
                    regroup[pl.ds(row, 8), n * BLOCK : (n + 1) * BLOCK] = tile_value
            return 0

        lax.fori_loop(0, 4, tile, 0)
        gathered[q, h] = regroup[...].astype(BF16)
        for k, sem in ((1, left_recv), (3, right_recv)):
            pltpu.make_async_remote_copy(
                src_ref=gathered.at[q, h], dst_ref=gathered.at[q, h], send_sem=ring_send, recv_sem=sem.at[h],
                device_id=device(g, other(k)), device_id_type=MESH,
            ).start()

    split = gathered.shape[2] // 2

    def forward(h):
        for origin, target, sem, far in ((3, 1, left_recv, 0), (1, 3, right_recv, 1)):
            whole = gathered.at[other(origin), h]
            pltpu.make_async_copy(whole, whole, sem.at[h]).wait()
            some = gathered.at[other(origin), h, pl.ds(far * split, split)]
            pltpu.make_async_remote_copy(
                src_ref=some, dst_ref=some, send_sem=ring_send, recv_sem=far_recv.at[far, h],
                device_id=device(g, other(target)), device_id_type=MESH,
            ).start()

    regroup_chunk(0)
    regroup_chunk(1)
    forward(0)

    pltpu.make_async_copy(near, near, out_recv).wait()
    half_from[...] = near[:2].astype(BF16)
    for side in range(2):
        pltpu.make_async_remote_copy(
            src_ref=half_from, dst_ref=near_half.at[side], send_sem=half_send, recv_sem=half_recv,
            device_id=device(beside(1 - 2 * side), q), device_id_type=MESH,
        ).start()
    regroup_chunk(2)
    forward(1)
    regroup_chunk(3)
    for h in range(2):
        for c in range(tcols):
            cols = slice(c * BLOCK, (c + 1) * BLOCK)
            temp_out[h * 8 : (h + 1) * 8, cols] = near[h, c * 8 : (c + 1) * 8, :]
            salt_out[h * 8 : (h + 1) * 8, cols] = near[2 + h, c * 8 : (c + 1) * 8, :]

    columns = nlev * gathered.shape[2]
    each = columns // 4
    at = lax.broadcasted_iota(jnp.int32, (columns, 1), 0)
    s = sum((at >= n * each).astype(jnp.int32) for n in range(1, 4))
    rest = at - s * each
    lev_rows = 4 * levels
    from_q = sum((rest >= n * lev_rows).astype(jnp.int32) for n in range(1, nlev))
    rest = rest - from_q * lev_rows
    lev = rest // 4
    f, c = (rest // 2) % 2, rest % 2
    want = from_q * (16 * levels) + (f * levels + lev) * 8 + c * 4 + s
    perm = jnp.where(want == lax.broadcasted_iota(jnp.int32, (columns, columns), 1), 1.0, 0.0).astype(BF16)

    def contract(h):
        for far in range(2):
            some = gathered.at[other(2), h, pl.ds(far * split, split)]
            pltpu.make_async_copy(some, some, far_recv.at[far, h]).wait()
        whole = jnp.concatenate([gathered[k, h] for k in range(nlev)], axis=0)
        ordered = jnp.dot(perm, whole, preferred_element_type=F32).astype(BF16)
        source = (high_at + 4 - h) % 4
        depth = section * band
        for s in range(4):
            term = jnp.dot(
                ordered[s * each : (s + 1) * each],
                leg[s, pl.ds(pl.multiple_of(source * depth, BLOCK), depth), :],
                preferred_element_type=F32,
            )
            spectra_ref[s] = term if h == 0 else spectra_ref[s] + term

    forward(2)
    leg_copy.wait()
    contract(0)
    forward(3)
    contract(1)

    pltpu.make_async_copy(near_half, near_half, half_recv).wait()
    mine = jnp.broadcast_to(slot_own[...].astype(F32), (BLOCK, per_lev)).T[:, :1]
    tiles = lax.broadcasted_iota(jnp.int32, (per_lev, part_rows), 1).astype(F32)
    surface = None
    for sec in range(3):
        for h in range(2):
            hot = jnp.where(mine == tiles + float((sec * 2 + h) * part_rows), 1.0, 0.0).astype(BF16)
            cells = near[h].astype(BF16) if sec == 1 else near_half[sec // 2, h]
            term = jnp.dot(hot, cells, preferred_element_type=F32)
            surface = term if surface is None else surface + term
    first_lane = lax.broadcasted_iota(jnp.int32, (band, BLOCK), 1)
    for b in range(lane_blocks):
        points = first_lane + (q * lane_blocks + b) * BLOCK
        base = (b // 3) * BLOCK + (b % 3) * band
        surface_ref[:, b * BLOCK : (b + 1) * BLOCK] = jnp.where(
            points < lat_col[:band, :], surface[base : base + band], 0.0
        )

    stores = [
        pltpu.make_async_copy(a, b, store_sem.at[n])
        for n, (a, b) in enumerate(
            ((temp_out, temp_to), (salt_out, salt_to), (surface_ref, surface_to), (spectra_ref, spectra_hbm))
        )
    ]
    for store in stores[:3]:
        store.start()
    contract(2)
    contract(3)
    stores[3].start()
    for store in stores:
        store.wait()

    for k in range(1, nlev):
        pltpu.make_async_copy(slot_own, slots.at[k], slot_send).wait()
    some = msg.at[pl.ds(0, groups - 1)]
    pltpu.make_async_copy(some, some, a2a_send).wait()
    for k in range(3 * nlev - 1):
        pltpu.make_async_copy(parts.at[0, 0], sums.at[0, 0], part_send).wait()
    three = gathered.at[pl.ds(0, 3)]
    pltpu.make_async_copy(three, three, ring_send).wait()
    for k in range(1, nlev):
        pltpu.make_async_copy(fresh, near.at[0], out_send).wait()
    for side in range(2):
        pltpu.make_async_copy(half_from, near_half.at[0], half_send).wait()


def store_kernel(*refs):
    count = len(refs) // 2
    for n in range(count):
        refs[count + n][...] = refs[n][...]


def body(
    sizes,
    atmos_fields,
    lat_points,
    wave_order,
    legendre,
    column_weight,
    block_remap,
    ocean_temp,
    ocean_salt,
    sea_mask,
):
    nlat, nlev, nocn = sizes
    nf, nl, band, length = atmos_fields.shape
    groups = nlat * nocn
    rows = nf * nl * band
    waves = wave_order.shape[0]
    orow, ocols = ocean_temp.shape
    part_rows = orow * ocols // BLOCK // 2
    each, nj, degrees = legendre.shape
    depth = nj // 4
    quarter = length // nlev
    lanes = rows // (3 * band) * BLOCK
    per_lev = -(-(quarter // BLOCK) // 3) * BLOCK
    steps = length // CHUNK
    hbm = pl.BlockSpec(memory_space=pltpu.HBM)
    sem = pltpu.SemaphoreType.DMA
    outs = [
        jax.ShapeDtypeStruct((each, nlev * nl * nf * 2, degrees), F32),
        jax.ShapeDtypeStruct((orow, ocols), F32),
        jax.ShapeDtypeStruct((orow, ocols), F32),
        jax.ShapeDtypeStruct((band, quarter), F32),
    ]
    results = pl.pallas_call(
        functools.partial(fused_kernel, sizes),
        in_specs=[hbm] * 9,
        out_specs=[hbm] * 4,
        out_shape=outs,
        scratch_shapes=[pltpu.VMEM(o.shape, F32) for o in outs]
        + [
            sem((4,)),
            pltpu.SMEM((band,), jnp.int32),
            pltpu.VMEM((1, waves), jnp.int32),
            pltpu.VMEM(column_weight.shape, BF16),
            pltpu.VMEM(block_remap.shape[::-1], jnp.int32),
            pltpu.VMEM((steps, rows, CHUNK), BF16),
            pltpu.VMEM((orow, ocols), F32),
            pltpu.VMEM((orow, ocols), F32),
            pltpu.VMEM(sea_mask.shape, jnp.int32),
            pltpu.VMEM(legendre.shape, BF16),
            pltpu.VMEM((CHUNK, 2 * waves), BF16),
            pltpu.VMEM((CHUNK, 2 * waves), BF16),
            pltpu.VMEM((rows, 2 * waves), F32),
            pltpu.VMEM((lanes, 2 * waves), F32),
            pltpu.VMEM((nlev * per_lev, 2 * BLOCK), F32),
            pltpu.VMEM((nlev * per_lev, 4 * BLOCK), BF16),
            pltpu.VMEM((2, BLOCK, waves), F32),
            pltpu.VMEM((2, length // BLOCK, waves), F32),
            pltpu.VMEM((2 * band, BLOCK), jnp.int32),
            pltpu.VMEM((16, BLOCK), F32),
            pltpu.VMEM((1, per_lev), jnp.int32),
            pltpu.VMEM((groups, 2 * each, lanes), BF16),
            pltpu.VMEM((groups, 2 * each, lanes), BF16),
            pltpu.VMEM((nlev, 4, nl * nf * 8, depth), BF16),
            pltpu.VMEM((nl * nf * 8, depth), F32),
            pltpu.VMEM((3, nlev, part_rows, BLOCK), BF16),
            pltpu.VMEM((3, nlev, part_rows, BLOCK), BF16),
            pltpu.VMEM((nlev, 1, per_lev), jnp.int32),
            pltpu.VMEM((1, ocols), F32),
            pltpu.VMEM((1, ocols), F32),
            pltpu.VMEM((part_rows, BLOCK), F32),
            pltpu.VMEM((nlev, part_rows, BLOCK), F32),
            pltpu.VMEM((2, part_rows, BLOCK), BF16),
            pltpu.VMEM((2, 2, part_rows, BLOCK), BF16),
            sem((7,)), sem((steps,)), sem, sem, sem((4,)), sem, sem, sem, sem, sem, sem,
            sem, sem((4,)), sem((4,)), sem((2, 4)), sem, sem, sem, sem,
        ],
        compiler_params=pltpu.CompilerParams(
            collective_id=0, has_side_effects=True, vmem_limit_bytes=62 * 1024 * 1024
        ),
    )(
        lat_points, wave_order.reshape(1, waves), column_weight, block_remap.T, atmos_fields.reshape(rows, length),
        ocean_temp, ocean_salt, sea_mask, legendre,
    )
    return pl.pallas_call(store_kernel, out_shape=outs)(*results)


def solution(mesh):
    both = ("lat", "ocn")
    placed = (
        P(None, "lev", both, None),
        P(both),
        P(),
        P(both, None, "lev"),
        P(None, "lev"),
        P(both, "lev"),
        P(both, None),
        P(both, None),
        P(both, None),
    )
    sizes = tuple(mesh.shape[a] for a in ("lat", "lev", "ocn"))
    return jax.shard_map(
        functools.partial(body, sizes),
        mesh=mesh,
        in_specs=placed,
        out_specs=(P(both, None, "lev"), P(both, None), P(both, None), P(both, "lev")),
        check_vma=False,
    )
```

time: 78.8 us -> 54 us (0.69); the launches traced: 77.3 us -> 53.9 us
  local copies, waits for them, and re-layouts: 14.9 us -> 0 us
  Pallas kernels: 60.9 us -> 53.3 us
    unnamed x20 -> x0, local copies, waits for them, and re-layouts: 13.3 us -> none
    pallas_call x2, Pallas kernels: 60.9 us -> 53.3 us  [the longest x1 51.1 us: body(): pl.pallas_call(functools.partial(fused_kernel, sizes), in_specs=[hbm] * 9...]
    reshape x3 -> x0, local copies, waits for them, and re-layouts: 1.56 us -> none  [the longest x1 0.74 us: body(): lat_points.reshape(band, 1)]
where the time goes in v3:
time: 54 us; the launch traced here: 53.9 us
  Pallas kernels  53.3 us (99%)
  between operations  0.64 us (1%)
    pallas_call x1, Pallas kernels, body(): pl.pallas_call(functools.partial(fused_kernel, sizes), in_specs=[hbm] * 9...  51.1 us
    pallas_call x1, Pallas kernels, body(): return pl.pallas_call(store_kernel, out_shape=outs)(*results)  2.22 us

profile of v3, /device:TPU:32, one launch (start us, length us, event | category | flops | bytes accessed | tf_op | source)
XLA Modules:
  0.0 53.9 jit_solution(10395585145369328703)
XLA Ops:
  0.6 51.1 %shard_map.120 = (f32[4,96,384]{2,1,0:T(8,128)}, f32[16,2176]{1,0:T(8,128)}, f32[16,2176]{1,0:T(8,128)}, f32[40,1408]{1,0:T(8,128)}) custom-call(s32[40]{0:T(128)} %lat_hbm.1, s32[1,256]{1,0:T(1,128)} %bitcast.5, bf16[2,6]{1,0:T(2,128)(2,1)} %weight_hbm.1, s32[11,40]{1,0:T(8,128)} %bitcast.4, bf16[480,5632]{1,0:T(8,128)(2,1)} %bitcast.3, ...), custom_call_target="tpu_custom_call" | custom-call | tf_op jit(solution)/shard_map/pallas_call | solution.py:513
  51.7 2.2 %shard_map.121 = (f32[4,96,384]{2,1,0:T(8,128)}, f32[16,2176]{1,0:T(8,128)}, f32[16,2176]{1,0:T(8,128)}, f32[40,1408]{1,0:T(8,128)}) custom-call(f32[4,96,384]{2,1,0:T(8,128)} %get-tuple-element.8.refs_0_, f32[16,2176]{1,0:T(8,128)} %get-tuple-element.9.refs_1_, f32[16,2176]{1,0:T(8,128)} %get-tuple-element.10.refs_2_, f32[40,1408]{1,0:T(8,128)} %get-tuple-element.11.refs_3_), custom_call_target="tpu_custom_call" | custom-call | tf_op jit(solution)/shard_map/pallas_call | solution.py:564

commit v4 on v3

--- a/solution.py
+++ b/solution.py
@@ -54,7 +54,8 @@
     lat_at, q, ocn_at = lax.axis_index("lat"), lax.axis_index("lev"), lax.axis_index("ocn")
     g = lat_at * nocn + ocn_at
     section = groups // 4
-    high_at, low_at = g // section, g % section
+    lat_section = nlat // 4
+    high_at, low_lat = lax.div(lat_at, lat_section), lax.rem(lat_at, lat_section)
     band = lat_hbm.shape[0]
     steps, rows, width = x_ref.shape
     waves = wave_ref.shape[1]
@@ -66,14 +67,20 @@
     count = length // BLOCK
     lane_blocks = count // nlev
 
-    def device(group, lev):
-        return (group // nocn, lev, group % nocn)
-
-    def beside(offset):
-        return (g + groups + offset) % groups
+    around = {-1: lax.rem(g + groups - 1, groups), 0: g, 1: lax.rem(g + 1, groups)}
+    place = {n: (lax.div(v, nocn), lax.rem(v, nocn)) for n, v in around.items()}
+    others = [lax.rem(q + k, nlev) for k in range(nlev)]
+    ocns = [lax.rem(ocn_at + o, nocn) for o in range(nocn)]
+
+    def beside(offset, lev):
+        lat, ocn = place[offset]
+        return (lat, lev, ocn)
+
+    def across(up):
+        return (jnp.where(up, place[1][0], place[-1][0]), q, jnp.where(up, place[1][1], place[-1][1]))
 
     def other(k):
-        return (q + k) % nlev
+        return others[k]
 
     small = [
         pltpu.make_async_copy(a, b, small_sem.at[n])
@@ -98,18 +105,21 @@
 
     lax.fori_loop(0, steps, start_x, 0)
     leg_copy = pltpu.make_async_copy(leg_hbm, leg, leg_sem)
-    leg_copy.start()
 
     barrier = pltpu.get_barrier_semaphore()
 
-    def greet(k, _):
-        pl.semaphore_signal(barrier, inc=1, device_id=device((g + k) % groups, q), device_id_type=MESH)
+    def greet(i, _):
+        lat = lax.rem(lat_at + i, nlat)
+        for o in range(nocn):
+            pl.semaphore_signal(barrier, inc=1, device_id=(lat, q, ocns[o]), device_id_type=MESH)
         return 0
 
-    lax.fori_loop(1, groups, greet, 0)
+    for o in range(1, nocn):
+        pl.semaphore_signal(barrier, inc=1, device_id=(lat_at, q, ocns[o]), device_id_type=MESH)
+    lax.fori_loop(1, nlat, greet, 0)
     for k in range(1, nlev):
         for offset in (-1, 0, 1):
-            pl.semaphore_signal(barrier, inc=1, device_id=device(beside(offset), other(k)), device_id_type=MESH)
+            pl.semaphore_signal(barrier, inc=1, device_id=beside(offset, other(k)), device_id_type=MESH)
 
     for copy in small:
         copy.wait()
@@ -195,7 +205,7 @@
     for k in range(1, nlev):
         pltpu.make_async_remote_copy(
             src_ref=slot_own, dst_ref=slots.at[q], send_sem=slot_send, recv_sem=slot_recv,
-            device_id=device(g, other(k)), device_id_type=MESH,
+            device_id=beside(0, other(k)), device_id_type=MESH,
         ).start()
     pltpu.make_async_copy(slot_own, slots.at[q], slot_recv).start()
     is_temp = q < 2
@@ -207,11 +217,12 @@
     )
     edge = pltpu.make_async_remote_copy(
         src_ref=edge_from, dst_ref=edge_to, send_sem=edge_send, recv_sem=edge_recv,
-        device_id=device(beside(1 - 2 * half), q), device_id_type=MESH,
+        device_id=across(half == 0), device_id_type=MESH,
     )
     edge.start()
 
     lax.fori_loop(early, steps, mask_step, 0)
+    leg_copy.start()
 
     high = blocks[...].astype(BF16)
     block_pair[:, : 2 * BLOCK] = high
@@ -231,7 +242,7 @@
                 continue
             pltpu.make_async_remote_copy(
                 src_ref=parts.at[sec, other(k)], dst_ref=sums.at[sec, q], send_sem=part_send, recv_sem=part_recv,
-                device_id=device(beside(sec - 1), other(k)), device_id_type=MESH,
+                device_id=beside(sec - 1, other(k)), device_id_type=MESH,
             ).start()
     pltpu.make_async_copy(parts.at[1, q], sums.at[1, q], part_recv).start()
 
@@ -275,17 +286,28 @@
     odd = jnp.where(first, pltpu.roll(real, 4, 1), imag)
     msg[...] = jnp.stack([even, odd], axis=1).reshape(msg.shape).astype(BF16)
 
-    for h in range(4):
-        def send(i, _, h=h):
-            target = ((high_at + h) % 4) * section + (low_at + i) % section
-            pltpu.make_async_remote_copy(
-                src_ref=msg.at[target], dst_ref=arrived.at[g], send_sem=a2a_send, recv_sem=a2a_recv.at[h],
-                device_id=device(target, q), device_id_type=MESH,
-            ).start()
-            return 0
-
-        lax.fori_loop(1 if h == 0 else 0, section, send, 0)
+    def send_group(n):
+        h, first = n // 2, n % 2 * (lat_section // 2)
+        high = lax.rem(high_at + h, 4)
+        for a in range(first, first + lat_section // 2):
+            lat_to = high * lat_section + lax.rem(low_lat + a, lat_section)
+            for o in range(nocn):
+                if h or a or o:
+                    pltpu.make_async_remote_copy(
+                        src_ref=msg.at[lat_to * nocn + ocns[o]], dst_ref=arrived.at[g],
+                        send_sem=a2a_send.at[n], recv_sem=a2a_recv.at[h],
+                        device_id=(lat_to, q, ocns[o]), device_id_type=MESH,
+                    ).start()
+
+    def wait_group(n):
+        some = msg.at[pl.ds(0, section // 2 - (n == 0))]
+        pltpu.make_async_copy(some, some, a2a_send.at[n]).wait()
+
     pltpu.make_async_copy(msg.at[g], arrived.at[g], a2a_recv.at[0]).start()
+    send_group(0)
+    send_group(1)
+    send_group(2)
+    send_group(3)
 
     pltpu.make_async_copy(sums, sums, part_recv).wait()
     forcing = None
@@ -319,14 +341,14 @@
     for k in range(1, nlev):
         pltpu.make_async_remote_copy(
             src_ref=fresh, dst_ref=near.at[q], send_sem=out_send, recv_sem=out_recv,
-            device_id=device(g, other(k)), device_id_type=MESH,
+            device_id=beside(0, other(k)), device_id_type=MESH,
         ).start()
     pltpu.make_async_copy(fresh, near.at[q], out_recv).start()
 
     lanes = lax.broadcasted_iota(jnp.int32, (8, BLOCK), 1)
 
     def regroup_chunk(h):
-        source = (high_at + 4 - h) % 4
+        source = lax.rem(high_at + 4 - h, 4)
         here = arrived.at[pl.ds(source * section, section)]
         pltpu.make_async_copy(here, here, a2a_recv.at[h]).wait()
 
@@ -355,7 +377,7 @@
         for k, sem in ((1, left_recv), (3, right_recv)):
             pltpu.make_async_remote_copy(
                 src_ref=gathered.at[q, h], dst_ref=gathered.at[q, h], send_sem=ring_send, recv_sem=sem.at[h],
-                device_id=device(g, other(k)), device_id_type=MESH,
+                device_id=beside(0, other(k)), device_id_type=MESH,
             ).start()
 
     split = gathered.shape[2] // 2
@@ -367,10 +389,18 @@
             some = gathered.at[other(origin), h, pl.ds(far * split, split)]
             pltpu.make_async_remote_copy(
                 src_ref=some, dst_ref=some, send_sem=ring_send, recv_sem=far_recv.at[far, h],
-                device_id=device(g, other(target)), device_id_type=MESH,
+                device_id=beside(0, other(target)), device_id_type=MESH,
             ).start()
 
+    wait_group(0)
+    send_group(4)
+    wait_group(1)
+    send_group(5)
     regroup_chunk(0)
+    wait_group(2)
+    send_group(6)
+    wait_group(3)
+    send_group(7)
     regroup_chunk(1)
     forward(0)
 
@@ -379,7 +409,7 @@
     for side in range(2):
         pltpu.make_async_remote_copy(
             src_ref=half_from, dst_ref=near_half.at[side], send_sem=half_send, recv_sem=half_recv,
-            device_id=device(beside(1 - 2 * side), q), device_id_type=MESH,
+            device_id=beside(1 - 2 * side, q), device_id_type=MESH,
         ).start()
     regroup_chunk(2)
     forward(1)
@@ -409,7 +439,7 @@
             pltpu.make_async_copy(some, some, far_recv.at[far, h]).wait()
         whole = jnp.concatenate([gathered[k, h] for k in range(nlev)], axis=0)
         ordered = jnp.dot(perm, whole, preferred_element_type=F32).astype(BF16)
-        source = (high_at + 4 - h) % 4
+        source = lax.rem(high_at + 4 - h, 4)
         depth = section * band
         for s in range(4):
             term = jnp.dot(
@@ -459,8 +489,10 @@
 
     for k in range(1, nlev):
         pltpu.make_async_copy(slot_own, slots.at[k], slot_send).wait()
-    some = msg.at[pl.ds(0, groups - 1)]
-    pltpu.make_async_copy(some, some, a2a_send).wait()
+    wait_group(4)
+    wait_group(5)
+    wait_group(6)
+    wait_group(7)
     for k in range(3 * nlev - 1):
         pltpu.make_async_copy(parts.at[0, 0], sums.at[0, 0], part_send).wait()
     three = gathered.at[pl.ds(0, 3)]
@@ -551,7 +583,7 @@
             pltpu.VMEM((nlev, part_rows, BLOCK), F32),
             pltpu.VMEM((2, part_rows, BLOCK), BF16),
             pltpu.VMEM((2, 2, part_rows, BLOCK), BF16),
-            sem((7,)), sem((steps,)), sem, sem, sem((4,)), sem, sem, sem, sem, sem, sem,
+            sem((7,)), sem((steps,)), sem, sem((8,)), sem((4,)), sem, sem, sem, sem, sem, sem,
             sem, sem((4,)), sem((4,)), sem((2, 4)), sem, sem, sem, sem,
         ],
         compiler_params=pltpu.CompilerParams(

time: 54 us -> 53.3 us (0.987); the launches traced: 53.9 us -> 52.3 us
  Pallas kernels: 53.3 us -> 51.7 us
    pallas_call x1, Pallas kernels: 51.1 us -> 49.5 us  [body(): pl.pallas_call(functools.partial(fused_kernel, sizes), in_specs=[hbm] * 9...]
where the time goes in v4:
time: 53.3 us; the launch traced here: 52.3 us
  Pallas kernels  51.7 us (97%)
  between operations  0.64 us (1%)
    pallas_call x1, Pallas kernels, body(): pl.pallas_call(functools.partial(fused_kernel, sizes), in_specs=[hbm] * 9...  49.5 us
    pallas_call x1, Pallas kernels, body(): return pl.pallas_call(store_kernel, out_shape=outs)(*results)  2.22 us

profile of v4, /device:TPU:32, one launch (start us, length us, event | category | flops | bytes accessed | tf_op | source)
XLA Modules:
  0.0 52.3 jit_solution(3409048411066333824)
XLA Ops:
  0.6 49.5 %shard_map.120 = (f32[4,96,384]{2,1,0:T(8,128)}, f32[16,2176]{1,0:T(8,128)}, f32[16,2176]{1,0:T(8,128)}, f32[40,1408]{1,0:T(8,128)}) custom-call(s32[40]{0:T(128)} %lat_hbm.1, s32[1,256]{1,0:T(1,128)} %bitcast.5, bf16[2,6]{1,0:T(2,128)(2,1)} %weight_hbm.1, s32[11,40]{1,0:T(8,128)} %bitcast.4, bf16[480,5632]{1,0:T(8,128)(2,1)} %bitcast.3, ...), custom_call_target="tpu_custom_call" | custom-call | tf_op jit(solution)/shard_map/pallas_call | solution.py:545
  50.1 2.2 %shard_map.121 = (f32[4,96,384]{2,1,0:T(8,128)}, f32[16,2176]{1,0:T(8,128)}, f32[16,2176]{1,0:T(8,128)}, f32[40,1408]{1,0:T(8,128)}) custom-call(f32[4,96,384]{2,1,0:T(8,128)} %get-tuple-element.8.refs_0_, f32[16,2176]{1,0:T(8,128)} %get-tuple-element.9.refs_1_, f32[16,2176]{1,0:T(8,128)} %get-tuple-element.10.refs_2_, f32[40,1408]{1,0:T(8,128)} %get-tuple-element.11.refs_3_), custom_call_target="tpu_custom_call" | custom-call | tf_op jit(solution)/shard_map/pallas_call | solution.py:596
